TPU v7x, 32 devices: a whole 2x2x4 slice. The times are simulated.
32 devices in a mesh: wave: 8 (over z, x), lev: 4 (over y, core).
Axes of the slice: x: 2, y: 2, z: 4, core: 2. Of those that a mesh axis runs over, the one named last changes fastest.
Arguments:
- grid: float32 [4, 640, 1344], P(None, 'lev', 'wave'), may hold values from -6 to 6
- row_points: int32 [640], replicated, may hold values from 20 to 1344, as said below
- lat_of_slot: int32 [640], replicated, may hold values from 0 to 639, each once
- pair_low: int32 [320], replicated, may hold values from 0 to 319, each once
- legendre: float32 [320, 205120], P(None, 'wave'), may hold values from -6 to 6
- lat_weight: float32 [320], replicated, may hold values from 0.02 to 0.2
- vert_modes: float32 [4, 4], replicated, may hold values from -3 to 3
- vert_back: float32 [4, 4], replicated, may hold values from -3 to 3
- vert_rates: float32 [4], replicated, may hold values from 0.5 to 20
Outputs:
- spectral: float32 [4, 2, 205824], P('lev', None, 'wave')
- grid_out: float32 [4, 640, 1344], P(None, 'lev', 'wave')
Inputs may be any that keep to these rules, and one draw needn't show every extreme that they name: row_points[r] is the number of points of the row of latitude r; it is even and equal to row_points[639 - r]. A permutation: row slot s holds latitude lat_of_slot[s]. A permutation: pair position g holds wavenumbers pair_low[g] and 639 - pair_low[g].
All inputs are finite; a program needn't handle non-finite values.
Results may differ from a plain program's by a relative error of at most 0.000084.
Values sent between devices are 32-bit elements; how exact they have to be, the bound alone decides.
A program may use at most 256 MiB of HBM per device.

v0:
```python
import math

import jax
import jax.numpy as jnp
from jax import lax
from jax.sharding import PartitionSpec as P

TWO_PI = 2.0 * math.pi
PRECISE = lax.Precision.HIGHEST
BLOCK_COLS = 128


def row_tables(row_length, inner_len, outer_len, waves):
    length_int = row_length[:, None, None]
    length_flt = length_int.astype(jnp.float32)
    wavenum = jnp.arange(waves, dtype=jnp.int32)[None, None, :]
    inner_idx = jnp.arange(inner_len, dtype=jnp.int32)[None, :, None]
    outer_idx = jnp.arange(outer_len, dtype=jnp.int32)[None, :, None]
    inner_angle = (wavenum * inner_idx % length_int).astype(jnp.float32) * TWO_PI / length_flt
    outer_angle = (
        (wavenum * (outer_idx * inner_len) % length_int).astype(jnp.float32) * TWO_PI / length_flt
    )
    return (jnp.cos(inner_angle), jnp.sin(inner_angle), jnp.cos(outer_angle), jnp.sin(outer_angle))


def wave_keep(row_length, waves):
    wavenum = jnp.arange(waves, dtype=jnp.int32)[None, :]
    keeper = (2 * wavenum < row_length[:, None]).astype(jnp.float32)
    return keeper * lax.rsqrt(row_length.astype(jnp.float32))[:, None]


def forward_dft(grid_rows, row_length, waves):
    vectors, row_count, length = grid_rows.shape
    inner_len = 32
    outer_len = length // inner_len
    live_mask = (jnp.arange(length, dtype=jnp.int32)[None, :] < row_length[:, None]).astype(
        jnp.float32
    )
    blocks = (grid_rows * live_mask[None]).reshape(vectors, row_count, outer_len, inner_len)
    cos_in, sin_in, cos_out, sin_out = row_tables(row_length, inner_len, outer_len, waves)
    first_real = jnp.einsum("vsoj,sjm->vsom", blocks, cos_in, precision=PRECISE)
    first_imaginary = -jnp.einsum("vsoj,sjm->vsom", blocks, sin_in, precision=PRECISE)
    fourier_real = jnp.sum(first_real * cos_out[None] + first_imaginary * sin_out[None], axis=2)
    fourier_imaginary = jnp.sum(
        first_imaginary * cos_out[None] - first_real * sin_out[None], axis=2
    )
    keeper = wave_keep(row_length, waves)[None]
    return (fourier_real * keeper, fourier_imaginary * keeper)


def inverse_dft(fourier_real, fourier_imaginary, row_length, length):
    vectors, row_count, waves = fourier_real.shape
    inner_len = 32
    outer_len = length // inner_len
    cos_in, sin_in, cos_out, sin_out = row_tables(row_length, inner_len, outer_len, waves)
    doubled = jnp.where(jnp.arange(waves, dtype=jnp.int32) == 0, 1.0, 2.0).astype(jnp.float32)
    weight_row = wave_keep(row_length, waves) * doubled[None, :]
    scaled_real = (fourier_real * weight_row[None])[:, :, None, :]
    scaled_imaginary = (fourier_imaginary * weight_row[None])[:, :, None, :]
    turned_real = scaled_real * cos_out[None] - scaled_imaginary * sin_out[None]
    turned_imaginary = scaled_real * sin_out[None] + scaled_imaginary * cos_out[None]
    values = jnp.einsum("vsom,sjm->vsoj", turned_real, cos_in, precision=PRECISE)
    values = values - jnp.einsum("vsom,sjm->vsoj", turned_imaginary, sin_in, precision=PRECISE)
    live_mask = (jnp.arange(length, dtype=jnp.int32)[None, :] < row_length[:, None]).astype(
        jnp.float32
    )
    return values.reshape(vectors, row_count, length) * live_mask[None]


def mode_degree(low_waves, waves):
    column = jnp.arange(waves + 1, dtype=jnp.int32)[None, :]
    low_length = (waves - low_waves)[:, None]
    return jnp.where(column < low_length, low_waves[:, None] + column, column - 1)


def column_order(low_waves, waves):
    column = jnp.arange(waves + 1, dtype=jnp.int32)[None, :]
    low_length = (waves - low_waves)[:, None]
    upper = (column >= low_length).astype(jnp.int32)
    parity = jnp.where(column >= low_length, column - low_length, column) % 2
    score = (parity * 2 + upper) * (waves + 1) + column
    order = jnp.argsort(score, axis=1)
    undo = jnp.argsort(order, axis=1)
    return (order, undo)


def padded_group(values, width):
    return jnp.pad(values, ((0, 0), (0, 0), (0, width - values.shape[2])))


def group_forward(inputs, leg_group, split):
    vectors, parts, lat_count, pair_count, _ = inputs.shape
    width = leg_group.shape[2]
    block_count = width // BLOCK_COLS
    starts = jnp.arange(block_count, dtype=jnp.int32) * BLOCK_COLS
    use_low = starts[None, :] < split[:, None]
    chosen = jnp.where(
        use_low[None, None, None], inputs[..., 0][..., None], inputs[..., 1][..., None]
    )
    leg_blocks = leg_group.reshape(lat_count, pair_count, block_count, BLOCK_COLS)
    main = jnp.einsum("vcigj,igjk->vcgjk", chosen, leg_blocks, precision=PRECISE).reshape(
        vectors, parts, pair_count, width
    )
    mixed = jnp.minimum(split // BLOCK_COLS, block_count - 1)
    leg_mixed = jnp.take_along_axis(leg_blocks, mixed[None, :, None, None], axis=2)[:, :, 0]
    extra = jnp.einsum("vcig,igk->vcgk", inputs[..., 1], leg_mixed, precision=PRECISE)
    extra_full = jnp.tile(extra, (1, 1, 1, block_count))
    column = jnp.arange(width, dtype=jnp.int32)[None, :]
    in_mixed = (column // BLOCK_COLS == mixed[:, None]) & (column >= split[:, None])
    return jnp.where(in_mixed[None, None], extra_full, main)


def group_back(coef, leg_group, split):
    vectors, parts, pair_count, width = coef.shape
    lat_count = leg_group.shape[0]
    block_count = width // BLOCK_COLS
    starts = jnp.arange(block_count, dtype=jnp.int32) * BLOCK_COLS
    use_low = starts[None, :] < split[:, None]
    column = jnp.arange(width, dtype=jnp.int32)[None, :]
    low_mask = (column < split[:, None]).astype(jnp.float32)
    coef_low = (coef * low_mask[None, None]).reshape(
        vectors, parts, pair_count, block_count, BLOCK_COLS
    )
    coef_high = (coef * (1.0 - low_mask)[None, None]).reshape(
        vectors, parts, pair_count, block_count, BLOCK_COLS
    )
    chosen = jnp.where(use_low[None, None, :, :, None], coef_low, coef_high)
    leg_blocks = leg_group.reshape(lat_count, pair_count, block_count, BLOCK_COLS)
    contrib = jnp.einsum("vcgjk,igjk->vcigj", chosen, leg_blocks, precision=PRECISE)
    low_weight = use_low.astype(jnp.float32)[None, None, None]
    to_low = jnp.sum(contrib * low_weight, axis=4)
    to_high = jnp.sum(contrib * (1.0 - low_weight), axis=4)
    mixed = jnp.minimum(split // BLOCK_COLS, block_count - 1)
    leg_mixed = jnp.take_along_axis(leg_blocks, mixed[None, :, None, None], axis=2)[:, :, 0]
    coef_mixed = jnp.take_along_axis(coef_high, mixed[None, None, :, None, None], axis=3)[
        :, :, :, 0
    ]
    flag = (mixed * BLOCK_COLS < split).astype(jnp.float32)
    extra = (
        jnp.einsum("vcgk,igk->vcig", coef_mixed, leg_mixed, precision=PRECISE)
        * flag[None, None, None]
    )
    return jnp.stack([to_low, to_high + extra], axis=-1)


def body(
    grid, row_points, lat_of_slot, pair_low, legendre, lat_weight, vert_modes, vert_back, vert_rates
):
    rows_in = lax.all_to_all(
        lax.all_to_all(grid, "lev", split_axis=0, concat_axis=1, tiled=True),
        "wave",
        split_axis=1,
        concat_axis=2,
        tiled=True,
    )
    lev_dev, lat_dev, points = rows_in.shape
    lat_total = lat_of_slot.shape[0]
    half_lat = lat_total // 2
    pair_count = legendre.shape[1] // (lat_total + 1)
    modes_used = pair_count * (lat_total + 1)
    modes_pad = (modes_used + 127) // 128 * 128
    even_count = lat_total // 2 + 1
    even_width = (even_count + BLOCK_COLS - 1) // BLOCK_COLS * BLOCK_COLS
    odd_width = (lat_total // 2 + BLOCK_COLS - 1) // BLOCK_COLS * BLOCK_COLS
    wave_index = lax.axis_index("wave")
    lev_index = lax.axis_index("lev")
    my_slots = lax.dynamic_slice_in_dim(lat_of_slot, wave_index * lat_dev, lat_dev)
    my_length = jnp.take(row_points, my_slots)
    my_low = lax.dynamic_slice_in_dim(pair_low, wave_index * pair_count, pair_count)
    wave_order = jnp.stack([pair_low, lat_total - 1 - pair_low], axis=1).reshape(lat_total)
    inverse_order = (
        jnp.zeros((lat_total,), jnp.int32)
        .at[wave_order]
        .set(jnp.arange(lat_total, dtype=jnp.int32))
    )
    slot_of_lat = (
        jnp.zeros((lat_total,), jnp.int32)
        .at[lat_of_slot]
        .set(jnp.arange(lat_total, dtype=jnp.int32))
    )
    order, undo = column_order(my_low, lat_total)
    split_even = (lat_total - my_low + 1) // 2
    split_odd = (lat_total - my_low) // 2
    legendre_cols = legendre.reshape(half_lat, pair_count, lat_total + 1)
    leg_sorted = jnp.take_along_axis(legendre_cols, order[None], axis=2)
    leg_even = padded_group(leg_sorted[:, :, :even_count], even_width)
    leg_odd = padded_group(leg_sorted[:, :, even_count:], odd_width)
    weight = lat_weight[None, None, :, None]
    fourier_real, fourier_imaginary = forward_dft(rows_in, my_length, lat_total)
    sorted_four = jnp.take(jnp.stack([fourier_real, fourier_imaginary], axis=1), wave_order, axis=3)
    arrived = lax.all_to_all(sorted_four, "wave", split_axis=3, concat_axis=2, tiled=True)
    items = arrived.shape[0]
    by_latitude = jnp.take(arrived, slot_of_lat, axis=2)
    north_rows = by_latitude[:, :, :half_lat]
    south_rows = jnp.flip(by_latitude[:, :, half_lat:], axis=2)
    symmetric = ((north_rows + south_rows) * weight).reshape(items, 2, half_lat, pair_count, 2)
    antisymmetric = ((north_rows - south_rows) * weight).reshape(items, 2, half_lat, pair_count, 2)
    even_out = group_forward(symmetric, leg_even, split_even)[..., :even_count]
    odd_out = group_forward(antisymmetric, leg_odd, split_odd)[..., : lat_total - even_count + 1]
    grouped = jnp.concatenate([even_out, odd_out], axis=3)
    spectra = jnp.take_along_axis(grouped, undo[None, None], axis=3).reshape(items, 2, modes_used)
    spectra = jnp.pad(spectra, ((0, 0), (0, 0), (0, modes_pad - modes_used)))
    degree = mode_degree(my_low, lat_total).reshape(modes_used).astype(jnp.float32)
    degree = jnp.pad(degree, (0, modes_pad - modes_used))
    eigen_term = degree * (degree + 1.0) / float(lat_total * lat_total)
    damping = 1.0 / (1.0 + vert_rates[:, None] * eigen_term[None, :])
    projected = jnp.einsum(
        "kj,jcm->kcm",
        vert_modes,
        lax.all_gather(spectra, "lev", axis=0, tiled=True),
        precision=PRECISE,
    )
    projected = projected * damping[:, None, :]
    own_rows = lax.dynamic_slice_in_dim(vert_back, lev_index * lev_dev, lev_dev, 0)
    solved = jnp.einsum("lk,kcm->lcm", own_rows, projected, precision=PRECISE)
    coefficients = solved[:, :, :modes_used].reshape(lev_dev, 2, pair_count, lat_total + 1)
    grouped = jnp.take_along_axis(coefficients, order[None, None], axis=3)
    coef_even = grouped[..., :even_count]
    coef_odd = grouped[..., even_count:]
    coef_even = jnp.pad(coef_even, ((0, 0), (0, 0), (0, 0), (0, even_width - coef_even.shape[3])))
    coef_odd = jnp.pad(coef_odd, ((0, 0), (0, 0), (0, 0), (0, odd_width - coef_odd.shape[3])))
    even_sum = group_back(coef_even, leg_even, split_even)
    odd_sum = group_back(coef_odd, leg_odd, split_odd)
    back_scale = 1.0 / math.sqrt(lat_total)
    north_rows = ((even_sum + odd_sum) * back_scale).reshape(lev_dev, 2, half_lat, 2 * pair_count)
    south_rows = ((even_sum - odd_sum) * back_scale).reshape(lev_dev, 2, half_lat, 2 * pair_count)
    whole_lat = jnp.concatenate([north_rows, jnp.flip(south_rows, axis=2)], axis=2)
    by_slot = jnp.take(whole_lat, lat_of_slot, axis=2)
    unsorted = jnp.take(
        lax.all_to_all(by_slot, "wave", split_axis=2, concat_axis=3, tiled=True),
        inverse_order,
        axis=3,
    )
    rows_out = inverse_dft(unsorted[:, 0], unsorted[:, 1], my_length, points)
    grid_out = lax.all_to_all(
        lax.all_to_all(rows_out, "wave", split_axis=2, concat_axis=1, tiled=True),
        "lev",
        split_axis=1,
        concat_axis=0,
        tiled=True,
    )
    return (solved, grid_out)


def solution(mesh):
    placed = (P(None, "lev", "wave"), P(), P(), P(), P(None, "wave"), P(), P(), P(), P())
    return jax.shard_map(
        body,
        mesh=mesh,
        in_specs=placed,
        out_specs=(P("lev", None, "wave"), P(None, "lev", "wave")),
        check_vma=False,
    )
```

profile of v0, /device:TPU:0, one launch (start us, length us, event | category | flops | bytes accessed | tf_op | source)
XLA Modules:
  0.0 2460.9 jit_solution(8594773094095567214)
XLA Ops:
  0.6 4.2 all-to-all-start
  18.3 4.1 scatter_custom_fusion
  27.2 17.9 sort.31
  49.5 17.3 sort.32
  67.0 40.0 %reshape.1365 = f32[320,40,641]{2,1,0:T(8,128)} reshape(f32[320,25640]{1,0:T(8,128)} %param.27) | data formatting | bytes 65638400 | tf_op jit(solution)/shard_map/reshape | solution.py:184
  107.0 41.5 %copy.353 = f32[320,40,641]{0,1,2:T(8,128)} copy(f32[320,40,641]{2,1,0:T(8,128)} %reshape.1365) | data formatting | bytes 65638400 | tf_op jit(solution)/shard_map/reshape | solution.py:184
  148.5 348.7 %gather_fusion.1 = f32[25640,320]{1,0:T(8,128)} fusion(f32[320,40,641]{0,1,2:T(8,128)} %copy.353, s32[25640]{0:T(1024)S(1)} %reshape.1491), kind=kCustom, calls=%fused_computation.11 | custom fusion | bytes 65843520 | tf_op jit(solution)/shard_map/jit(take_along_axis)/gather | solution.py:185
  497.3 36.5 %reshape.1595 = f32[40,641,320]{2,1,0:T(8,128)} reshape(f32[25640,320]{1,0:T(8,128)} %gather_fusion.1) | data formatting | bytes 65638400 | tf_op jit(solution)/shard_map/jit(take_along_axis)/gather | solution.py:185
  533.8 43.5 %copy.428 = f32[40,641,320]{1,0,2:T(8,128)} copy(f32[40,641,320]{2,1,0:T(8,128)} %reshape.1595) | data formatting | bytes 65638400 | tf_op jit(solution)/shard_map/jit(take_along_axis)/gather | solution.py:185
  578.8 13.8 select_bitcast_fusion
  592.7 8.2 slice_select_fusion
  600.9 10.7 copy-done.2
  615.0 7.2 all-to-all-start.1
  623.0 17.1 all-to-all-done.1
  643.0 103.7 %fusion.57 = f32[80,640,42]{1,2,0:T(8,128)S(1)} fusion(f32[80,42,32]{1,2,0:T(8,128)S(1)} %copy.361, f32[80]{0:T(128)S(1)} %copy-done.49, pred[80]{0:T(512)(128)(4,1)S(1)} %copy-done.47, s32[80]{0:T(128)S(1)} %copy-done.51, s32[32,640]{1,0:T(8,128)S(1)} %copy-done.22), kind=kOutput, calls=%fused_computation.77 | convolution fusion | flops 842137600 | bytes 9114320 | tf_op jit(solution)/shard_map/vsoj,sjm->vsom/dot_general | solution.py:42
  746.7 225.7 %fusion.5 = (f32[80,640]{1,0:T(8,128)S(1)}, f32[80,640]{1,0:T(8,128)S(1)}) fusion(f32[80,640,42]{1,2,0:T(8,128)S(1)} %fusion.57, f32[80]{0:T(128)S(1)} %copy-done.49, pred[80]{0:T(512)(128)(4,1)S(1)} %copy-done.47, s32[80]{0:T(128)S(1)} %copy-done.51, s32[42,640]{1,0:T(8,128)S(1)} %multiply_bitcast_fusion, f32[80,42,32]{1,2,0:T(8,128)S(1)} %copy.361, ...), kind=kOutput, calls=%fused_computation.32 | convolution fusion | flops 882892800 | bytes 9631440 | tf_op jit(solution)/shard_map/vsoj,sjm->vsom/dot_general | solution.py:41
  978.4 3.1 fusion.77
  981.5 3.6 all-to-all-start.2
  985.9 18.7 slice.104
  1004.9 21.4 copy.441
  1026.4 22.6 copy.355
  1049.0 15.5 pad.25.clone
  1064.5 12.3 gather_fusion.2
  1076.9 12.3 gather_fusion.5
  1095.1 28.7 %convolution_bitcast_fusion.3 = f32[1,2,40,3,128]{4,1,3,2,0:T(2,128)S(1)} fusion(f32[320,40,3,128]{0,3,2,1:T(8,128)} %bitcast.404, pred[40,3]{1,0:T(8,128)(4,1)S(1)} %copy-done.25, f32[2,320,40]{1,0,2:T(2,128)S(1)} %get-tuple-element.51, f32[2,320,40]{1,0,2:T(2,128)S(1)} %get-tuple-element.50), kind=kOutput, calls=%fused_computation.83 | convolution fusion | flops 118041600 | bytes 19988600 | tf_op jit(solution)/shard_map/vcigj,igjk->vcgjk/dot_general | solution.py:101
  1123.9 28.3 %convolution_bitcast_fusion.4 = f32[1,2,40,3,128]{4,1,3,2,0:T(2,128)S(1)} fusion(f32[320,40,3,128]{0,3,2,1:T(8,128)} %bitcast.399, pred[40,3]{1,0:T(8,128)(4,1)S(1)} %copy-done.24, f32[2,320,40]{1,0,2:T(2,128)S(1)} %get-tuple-element.49, f32[2,320,40]{1,0,2:T(2,128)S(1)} %get-tuple-element.48), kind=kOutput, calls=%fused_computation.84 | convolution fusion | flops 118041600 | bytes 19988600 | tf_op jit(solution)/shard_map/vcigj,igjk->vcgjk/dot_general | solution.py:101
  1152.4 11.3 fusion.72
  1163.8 11.1 fusion.69
  1175.2 7.8 copy.382
  1183.0 290.0 %gather_fusion.6 = f32[25640,2]{1,0:T(8,128)} fusion(f32[2,40,641]{0,1,2:T(8,128)} %bitcast.406, s32[25640]{0:T(1024)S(1)} %reshape.1558), kind=kCustom, calls=%fused_computation.3.clone | custom fusion | bytes 615360 | tf_op jit(solution)/shard_map/jit(take_along_axis)/gather | solution.py:201
  1472.9 7.8 copy.383
  1481.4 9.1 all_gather.3
  1494.7 7.8 copy.386
  1502.5 289.5 %gather_fusion.7 = f32[25640,2]{1,0:T(8,128)} fusion(f32[2,40,641]{0,1,2:T(8,128)} %bitcast.407, s32[25640]{0:T(1024)S(1)} %reshape.1565), kind=kCustom, calls=%fused_computation.8.clone | custom fusion | bytes 615360 | tf_op jit(solution)/shard_map/jit(take_along_axis)/gather | solution.py:217
  1792.0 7.8 copy.387
  1809.7 18.1 multiply_reduce_fusion.1
  1827.9 15.4 multiply_reduce_fusion.3
  1845.3 7.6 fusion.24
  1853.9 7.8 fusion.20
  1869.2 6.0 all-to-all-start.3
  1875.2 4.1 scatter_custom_fusion.1
  1879.3 13.8 all-to-all-done.3
  1900.1 152.3 %fusion.177 = f32[80,42,640]{2,1,0:T(8,128)S(1)} fusion(f32[80,640]{1,0:T(8,128)S(1)} %copy.411, f32[80,640]{1,0:T(8,128)S(1)} %copy.410, f32[80]{0:T(128)S(1)} %copy-done.50, pred[80]{0:T(512)(128)(4,1)S(1)} %copy-done.48, s32[80]{0:T(128)S(1)} %copy-done.52, s32[42,640]{1,0:T(8,128)S(1)} %multiply_bitcast_fusion), kind=kLoop, calls=%fused_computation.38.clone.2 | loop fusion | flops 27955200 | bytes 9119440 | tf_op jit(solution)/shard_map/vsom,sjm->vsoj/dot_general | solution.py:63
  2052.4 166.1 %fusion.179 = f32[80,42,640]{2,1,0:T(8,128)S(1)} fusion(f32[80,640]{1,0:T(8,128)S(1)} %copy.411, f32[80,640]{1,0:T(8,128)S(1)} %copy.410, f32[80]{0:T(128)S(1)} %copy-done.50, pred[80]{0:T(512)(128)(4,1)S(1)} %copy-done.48, s32[80]{0:T(128)S(1)} %copy-done.52, s32[42,640]{1,0:T(8,128)S(1)} %multiply_bitcast_fusion), kind=kLoop, calls=%fused_computation.42.clone.clone.clone.clone.clone.2 | loop fusion | flops 27955200 | bytes 9119440 | tf_op jit(solution)/shard_map/vsom,sjm->vsoj/dot_general | solution.py:62
  2218.4 108.7 %fusion.8 = f32[80,32,42]{2,1,0:T(8,128)S(1)} fusion(f32[80]{0:T(128)S(1)} %copy-done.50, pred[80]{0:T(512)(128)(4,1)S(1)} %copy-done.48, s32[80]{0:T(128)S(1)} %copy-done.52, s32[32,640]{1,0:T(8,128)S(1)} %copy-done.23, f32[80,42,640]{2,1,0:T(8,128)S(1)} %fusion.177), kind=kOutput, calls=%fused_computation.37 | convolution fusion | flops 842137600 | bytes 9114320 | tf_op jit(solution)/shard_map/vsom,sjm->vsoj/dot_general | solution.py:63
  2327.2 95.2 %fusion.64 = f32[1,80,42,32]{2,3,1,0:T(8,128)S(1)} fusion(f32[80,32,42]{2,1,0:T(8,128)S(1)} %fusion.8, f32[80]{0:T(128)S(1)} %copy-done.50, pred[80]{0:T(512)(128)(4,1)S(1)} %copy-done.48, s32[80]{0:T(128)S(1)} %copy-done.52, s32[32,640]{1,0:T(8,128)S(1)} %copy-done.23, f32[80,42,640]{2,1,0:T(8,128)S(1)} %fusion.179), kind=kOutput, calls=%fused_computation.79 | convolution fusion | flops 842245120 | bytes 9544400 | tf_op jit(solution)/shard_map/vsom,sjm->vsoj/dot_general | solution.py:62
  2423.6 21.9 all_to_all.96
  2446.9 12.7 all_to_all.97
  (313 shorter events, 79.6 us)
Async XLA Ops:
  0.6 611.7 %all-to-all-start = ((f32[4,160,168]{2,1,0:T(8,128)}), f32[4,160,168]{2,1,0:T(8,128)}, u32[]{:S(2)}, u32[]{:S(2)}) async-start(f32[4,160,168]{2,1,0:T(8,128)} %param.23), calls=%async_computation | async-start | bytes 1310720 | tf_op jit(solution)/shard_map/all_to_all | solution.py:150
  6.9 20.2 copy-start.34
  8.6 18.5 copy-start.36
  45.1 21.8 copy-start.3
  533.8 43.6 %copy-start.43 = (s32[40,2]{0,1:T(2,128)S(1)}, s32[40,2]{0,1:T(2,128)}, u32[]{:S(2)}) copy-start(s32[40,2]{0,1:T(2,128)} %get-tuple-element.72) | copy-start | bytes 964
  533.8 43.6 %copy-start.44 = (s32[40,2]{0,1:T(2,128)S(1)}, s32[40,2]{0,1:T(2,128)}, u32[]{:S(2)}) copy-start(s32[40,2]{0,1:T(2,128)} %get-tuple-element.74) | copy-start | bytes 964
  533.8 44.1 %copy-start.15 = (f32[25728]{0:T(1024)S(1)}, f32[25728]{0:T(1024)}, u32[]{:S(2)}) copy-start(f32[25728]{0:T(1024)} %fusion.102) | copy-start | bytes 308740
  533.8 44.1 %copy-start.66 = (f32[4]{0:T(128)S(1)}, f32[4]{0:T(128)}, u32[]{:S(2)}) copy-start(f32[4]{0:T(128)} %param.31) | copy-start | bytes 52
  533.8 45.0 %copy-start.20 = (pred[40,641]{1,0:T(8,128)(4,1)S(1)}, pred[40,641]{1,0:T(8,128)(4,1)}, u32[]{:S(2)}) copy-start(pred[40,641]{1,0:T(8,128)(4,1)} %compare_and_fusion) | copy-start | bytes 76924
  592.6 19.0 copy-start.2
  592.7 19.0 copy-start.30
  592.7 19.0 copy-start.37
  592.7 29.5 %copy-start.35 = (s32[40]{0:T(128)S(1)}, s32[40]{0:T(128)}, u32[]{:S(2)}) copy-start(s32[40]{0:T(128)} %copy-done.34) | copy-start | bytes 484
  592.7 30.2 %copy-start.14 = (s32[40,641]{1,0:T(8,128)S(1)}, s32[40,641]{1,0:T(8,128)}, u32[]{:S(2)}) copy-start(s32[40,641]{1,0:T(8,128)} %get-tuple-element.10) | copy-start | bytes 307684
  592.7 48.8 %copy-start.21 = (s32[42,32]{1,0:T(8,128)S(1)}, s32[42,32]{1,0:T(8,128)}, u32[]{:S(2)}) copy-start(s32[42,32]{1,0:T(8,128)} %multiply_add_fusion) | copy-start | bytes 16132
  592.7 48.8 %copy-start.32 = (s32[80]{0:T(128)S(1)}, s32[80]{0:T(128)}, u32[]{:S(2)}) copy-start(s32[80]{0:T(128)} %copy-done.31) | copy-start | bytes 964
  611.6 31.3 %copy-start.22 = (s32[32,640]{1,0:T(8,128)S(1)}, s32[32,640]{1,0:T(8,128)}, u32[]{:S(2)}) copy-start(s32[32,640]{1,0:T(8,128)} %multiply_bitcast_fusion.1) | copy-start | bytes 245764
  611.6 31.3 %copy-start.47 = (pred[80]{0:T(512)(128)(4,1)S(1)}, pred[80]{0:T(512)(128)(4,1)}, u32[]{:S(2)}) copy-start(pred[80]{0:T(512)(128)(4,1)} %compare_bitcast_fusion) | copy-start | bytes 244
  611.6 31.3 %copy-start.49 = (f32[80]{0:T(128)S(1)}, f32[80]{0:T(128)}, u32[]{:S(2)}) copy-start(f32[80]{0:T(128)} %convert_element_type.97) | copy-start | bytes 964
  611.6 31.4 %copy-start.51 = (s32[80]{0:T(128)S(1)}, s32[80]{0:T(128)}, u32[]{:S(2)}) copy-start(s32[80]{0:T(128)} %fusion.140) | copy-start | bytes 964
  615.0 25.1 %all-to-all-start.1 = ((f32[1,640,168]{2,0,1:T(1,128)}), f32[1,640,168]{2,0,1:T(1,128)S(1)}, u32[]{:S(2)}, u32[]{:S(2)}) async-start(f32[1,640,168]{2,0,1:T(1,128)} %copy.358), calls=%async_computation.1 | async-start | bytes 1310720 | tf_op jit(solution)/shard_map/all_to_all | solution.py:149
  746.7 226.1 %copy-start.26 = (s32[640]{0:T(1024)S(1)}, s32[640]{0:T(1024)}, u32[]{:S(2)}) copy-start(s32[640]{0:T(1024)} %iota_multiply_fusion) | copy-start | bytes 7684
  746.7 226.1 %copy-start.40 = (f32[80]{0:T(128)S(1)}, f32[80]{0:T(128)}, u32[]{:S(2)}) copy-start(f32[80]{0:T(128)} %get-tuple-element.40) | copy-start | bytes 964
  746.7 231.7 %copy-start.46 = (pred[640]{0:T(1024)(128)(4,1)S(1)}, pred[640]{0:T(1024)(128)(4,1)}, u32[]{:S(2)}) copy-start(pred[640]{0:T(1024)(128)(4,1)} %compare_and_fusion.4) | copy-start | bytes 1924
  746.7 238.5 %copy-start.7 = (s32[320,2]{1,0:T(8,128)S(1)}, s32[320,2]{1,0:T(8,128)}, u32[]{:S(2)}) copy-start(s32[320,2]{1,0:T(8,128)} %copy-done.6) | copy-start | bytes 7684
  981.5 108.5 %all-to-all-start.2 = ((f32[1,2,80,640]{2,1,0,3:T(2,128)}), f32[1,2,80,640]{2,1,0,3:T(2,128)S(1)}, u32[]{:S(2)}, u32[]{:S(2)}) async-start(f32[1,2,80,640]{2,1,0,3:T(2,128)} %fusion.77), calls=%async_computation.2 | async-start | bytes 1310720 | tf_op jit(solution)/shard_map/all_to_all | solution.py:191
  985.9 18.8 copy-start.13
  1095.1 28.8 %copy-start.24 = (pred[40,3]{1,0:T(8,128)(4,1)S(1)}, pred[40,3]{1,0:T(8,128)(4,1)}, u32[]{:S(2)}) copy-start(pred[40,3]{1,0:T(8,128)(4,1)} %get-tuple-element.63) | copy-start | bytes 364
  1123.9 28.4 %copy-start.53 = (pred[40]{0:T(512)(128)(4,1)S(1)}, pred[40]{0:T(512)(128)(4,1)}, u32[]{:S(2)}) copy-start(pred[40]{0:T(512)(128)(4,1)} %and_bitcast_fusion.5) | copy-start | bytes 124
  1123.9 39.9 %copy-start.55 = (pred[40]{0:T(512)(128)(4,1)S(1)}, pred[40]{0:T(512)(128)(4,1)}, u32[]{:S(2)}) copy-start(pred[40]{0:T(512)(128)(4,1)} %and_bitcast_fusion.4) | copy-start | bytes 124
  1494.4 297.6 %copy-start.10 = (f32[1,2,25728]{2,1,0:T(2,128)}, f32[1,2,25728]{2,1,0:T(2,128)S(1)}, u32[]{:S(2)}) copy-start(f32[1,2,25728]{2,1,0:T(2,128)S(1)} %copy.423) | copy-start | bytes 617476
  1800.3 27.5 %slice-start = ((s8[23592960]{0:T(1024)(128)(4,1)}), s8[2621440]{0:T(1024)(128)(4,1)S(1)}, s32[]{:S(2)}) async-start(s8[23592960]{0:T(1024)(128)(4,1)} %bitcast.400), calls=%async_computation.6 | async-start | bytes 5242880
  1827.9 25.1 %copy-start.8 = (s32[40]{0:T(128)S(1)}, s32[40]{0:T(128)}, u32[]{:S(2)}) copy-start(s32[40]{0:T(128)} %get-tuple-element.81) | copy-start | bytes 484
  1827.9 26.0 %copy-start.54 = (pred[40]{0:T(512)(128)(4,1)S(1)}, pred[40]{0:T(512)(128)(4,1)}, u32[]{:S(2)}) copy-start(pred[40]{0:T(512)(128)(4,1)} %and_bitcast_fusion.5) | copy-start | bytes 124
  1827.9 26.0 %copy-start.67 = (pred[40]{0:T(512)(128)(4,1)S(1)}, pred[40]{0:T(512)(128)(4,1)}, u32[]{:S(2)}) copy-start(pred[40]{0:T(512)(128)(4,1)} %and_bitcast_fusion.3) | copy-start | bytes 124
  1843.4 18.4 copy-start.58
  1843.4 18.5 copy-start.57
  1845.3 20.8 copy-start.45
  1852.9 22.2 copy-start.38
  1861.7 37.7 %copy-start.27 = (s32[640]{0:T(1024)S(1)}, s32[640]{0:T(1024)}, u32[]{:S(2)}) copy-start(s32[640]{0:T(1024)} %iota_multiply_fusion) | copy-start | bytes 7684
  1861.7 37.7 %copy-start.33 = (s32[80]{0:T(128)S(1)}, s32[80]{0:T(128)}, u32[]{:S(2)}) copy-start(s32[80]{0:T(128)} %copy-done.31) | copy-start | bytes 964
  1861.8 37.7 %copy-start.41 = (f32[80]{0:T(128)S(1)}, f32[80]{0:T(128)}, u32[]{:S(2)}) copy-start(f32[80]{0:T(128)} %get-tuple-element.40) | copy-start | bytes 964
  1861.8 38.3 %copy-start.48 = (pred[80]{0:T(512)(128)(4,1)S(1)}, pred[80]{0:T(512)(128)(4,1)}, u32[]{:S(2)}) copy-start(pred[80]{0:T(512)(128)(4,1)} %compare_bitcast_fusion) | copy-start | bytes 244
  1861.8 38.3 %copy-start.50 = (f32[80]{0:T(128)S(1)}, f32[80]{0:T(128)}, u32[]{:S(2)}) copy-start(f32[80]{0:T(128)} %convert_element_type.97) | copy-start | bytes 964
  1861.8 38.3 %copy-start.52 = (s32[80]{0:T(128)S(1)}, s32[80]{0:T(128)}, u32[]{:S(2)}) copy-start(s32[80]{0:T(128)} %fusion.140) | copy-start | bytes 964
  1869.2 23.9 all-to-all-start.3
  1900.1 318.4 %copy-start.23 = (s32[32,640]{1,0:T(8,128)S(1)}, s32[32,640]{1,0:T(8,128)}, u32[]{:S(2)}) copy-start(s32[32,640]{1,0:T(8,128)} %multiply_bitcast_fusion.1) | copy-start | bytes 245764
  2327.2 133.3 %copy-start.1 = (s32[640]{0:T(1024)S(1)}, s32[640]{0:T(1024)}, u32[]{:S(2)}) copy-start(s32[640]{0:T(1024)} %param.24) | copy-start | bytes 7684
  (31 other events, 433.3 us)
where the time goes:
time: 2480 us; the launch traced here: 2460 us
  local copies, waits for them, and re-layouts  1280 us (52%)
  matrix products  665 us (27%)
  other arithmetic  417 us (17%)
  blocking collectives  43.6 us (2%)
  waiting for transfers between devices  30.9 us (1%)
    gather x4, local copies, waits for them, and re-layouts, body(): leg_sorted = jnp.take_along_axis(legendre_cols, order[None], axis=2)  429 us
    gather x4, local copies, waits for them, and re-layouts, body(): jnp.take_along_axis(grouped, undo[None, None], axis=3)  298 us
    gather x4, local copies, waits for them, and re-layouts, body(): grouped = jnp.take_along_axis(coefficients, order[None, None], axis=3)  298 us
    dot_general x1, matrix products, forward_dft(): first_real = jnp.einsum('vsoj,sjm->vsom', blocks, cos_in, precision=PRECISE)  226 us
    dot_general x1, other arithmetic, inverse_dft(): jnp.einsum('vsom,sjm->vsoj', turned_real, cos_in, precision=PRECISE)  166 us
    dot_general x1, other arithmetic, inverse_dft(): jnp.einsum('vsom,sjm->vsoj', turned_imaginary, sin_in, precision=PRECISE)  152 us
    dot_general x1, matrix products, inverse_dft(): jnp.einsum('vsom,sjm->vsoj', turned_imaginary, sin_in, precision=PRECISE)  109 us
    dot_general x1, matrix products, forward_dft(): jnp.einsum('vsoj,sjm->vsom', blocks, sin_in, precision=PRECISE)  104 us
  transfers between devices with their start and end apart: 4, of which 2 were waited for; matrix products, arithmetic and copies ran while one was open for 29% of the time, Pallas kernels for 0%

commit v1 on v0

v1 whole, which is shorter than its diff:
```python
import functools
import math

import jax
import jax.numpy as jnp
import numpy as np
from jax import lax
from jax.experimental import pallas as pl
from jax.experimental.pallas import tpu as pltpu
from jax.sharding import PartitionSpec as P

HIGHEST = lax.Precision.HIGHEST
BOTH = ("wave", "lev")
INNER = 64
WIDTH = 512
NN = (((1,), (0,)), ((), ()))
NT = (((1,), (1,)), ((), ()))


def half_turn_fit():
    nodes = 0.5 * np.cos(np.pi * (np.arange(400) + 0.5) / 800)
    square = nodes**2
    sine = np.linalg.lstsq(
        np.vander(square, 5, increasing=True), np.sin(np.pi * nodes) / nodes, rcond=None
    )[0]
    cosine = np.linalg.lstsq(
        np.vander(square, 6, increasing=True), np.cos(np.pi * nodes), rcond=None
    )[0]
    return [round(float(c), 10) for c in sine], [round(float(c), 10) for c in cosine]


SINE, COSINE = half_turn_fit()


def poly(coefs, square):
    total = coefs[-1] * square + coefs[-2]
    for c in coefs[-3::-1]:
        total = total * square + c
    return total


def turn(product, length, inverse):
    rest = product - jnp.floor(product * inverse + 0.5) * length
    part = rest * inverse
    square = part * part
    sine = poly(SINE, square) * part
    cosine = poly(COSINE, square)
    double = sine + sine
    return 1.0 - double * sine, double * cosine


def halves(x):
    high = x.astype(jnp.bfloat16)
    return high, (x - high.astype(jnp.float32)).astype(jnp.bfloat16)


def both_halves(x):
    high = x.astype(jnp.bfloat16).astype(jnp.float32)
    return jnp.concatenate([high, x - high], axis=0).astype(jnp.bfloat16), high.astype(jnp.bfloat16)


def dot(a, b, dims):
    return lax.dot_general(a, b, dims, preferred_element_type=jnp.float32)


def dot_split(stacked, high, b_high, b_low, dims):
    rows = high.shape[0]
    first = dot(stacked, b_high, dims)
    return first[:rows] + first[rows:] + dot(high, b_low, dims)


def row_iota(rows):
    return lax.broadcasted_iota(jnp.int32, (rows, 1), 0)


def live_mask(length, vectors, outer):
    row = row_iota(vectors * outer) % outer
    position = row * INNER + lax.broadcasted_iota(jnp.int32, (vectors * outer, INNER), 1)
    return (position.astype(jnp.float32) < length).astype(jnp.float32)


def tables(wave, length, inverse, outer):
    inner_idx = row_iota(INNER).astype(jnp.float32)
    outer_idx = (row_iota(outer) * INNER).astype(jnp.float32)
    return turn(inner_idx * wave, length, inverse) + turn(outer_idx * wave, length, inverse)


def forward_kernel(vectors, outer, facts, x_ref, wave_ref, out_ref):
    def one(r, carry):
        length, inverse, norm = facts[0, r], facts[1, r], facts[2, r]
        wave = wave_ref[...]
        cos_in, sin_in, cos_out, sin_out = tables(wave, length, inverse, outer)
        x = x_ref[r] * live_mask(length, vectors, outer)
        stacked, high = both_halves(x)
        along = dot_split(stacked, high, *halves(cos_in), NN)
        across = dot_split(stacked, high, *halves(sin_in), NN)
        keep = jnp.where(wave + wave < length, norm, 0.0)
        rows = []
        for v in range(vectors):
            p, q = along[v * outer : (v + 1) * outer], across[v * outer : (v + 1) * outer]
            rows.append(jnp.sum(p * cos_out - q * sin_out, axis=0, keepdims=True) * keep)
            rows.append(jnp.sum(q * cos_out + p * sin_out, axis=0, keepdims=True) * -keep)
        out_ref[r] = jnp.concatenate(rows, axis=0)
        return carry

    lax.fori_loop(0, x_ref.shape[0], one, 0)


def inverse_kernel(vectors, outer, scale, facts, f_ref, wave_ref, out_ref):
    def one(r, carry):
        length, inverse, norm = facts[0, r], facts[1, r], facts[2, r]
        wave = wave_ref[...]
        cos_in, sin_in, cos_out, sin_out = tables(wave, length, inverse, outer)
        weight = jnp.where(wave + wave < length, norm * scale, 0.0)
        weight = weight * jnp.where(wave == 0.0, 1.0, 2.0)
        four = f_ref[r] * weight
        real, imaginary = [], []
        for v in range(vectors):
            a, b = four[2 * v : 2 * v + 1], four[2 * v + 1 : 2 * v + 2]
            real.append(a * cos_out - b * sin_out)
            imaginary.append(-(a * sin_out + b * cos_out))
        values = dot_split(*both_halves(jnp.concatenate(real, axis=0)), *halves(cos_in), NT)
        values += dot_split(*both_halves(jnp.concatenate(imaginary, axis=0)), *halves(sin_in), NT)
        out_ref[r] = values * live_mask(length, vectors, outer)
        return carry

    lax.fori_loop(0, f_ref.shape[0], one, 0)


def legendre_kernel(
    waves, used, span, place, low, four_ref, leg_ref, modes_ref, back_ref, rates_ref, spec_ref, out_ref
):
    step = pl.program_id(0)
    rows = four_ref.shape[1]
    fields = rows // 4
    pair_total = low.shape[0]
    first_pair = place[1]

    @pl.when(step == 0)
    def _():
        out_ref[...] = jnp.zeros_like(out_ref)

    base = (place[0] + step) * WIDTH
    pair = base // (waves + 1)
    column = base + lax.broadcasted_iota(jnp.int32, (1, WIDTH), 1)
    second = column >= (pair + 1) * (waves + 1)
    own_pair = jnp.where(second, pair + 1, pair)
    last = pair_total - 1
    low_wave = jnp.where(
        second, low[jnp.minimum(pair + 1, last)], low[jnp.minimum(pair, last)]
    )
    inside = column - own_pair * (waves + 1)
    low_length = waves - low_wave
    upper = inside >= low_length
    kind = jnp.where(upper, 2 + ((inside - low_length) & 1), inside & 1)
    degree = jnp.where(upper, inside - 1, low_wave + inside).astype(jnp.float32)
    valid = (own_pair >= first_pair) & (own_pair < first_pair + span) & (column < used)
    kind = jnp.where(valid, jnp.where(second, kind + 4, kind), 8)
    masks = [(kind == s).astype(jnp.float32) for s in range(8)]

    here = jnp.clip(pair - first_pair, 0, span - 1)
    there = jnp.clip(pair + 1 - first_pair, 0, span - 1)
    leg = jnp.where(column < used, leg_ref[...], 0.0)
    leg_high, leg_low = halves(leg)
    four = jnp.concatenate([four_ref[here], four_ref[there]], axis=0)
    product = dot_split(*both_halves(four), leg_high, leg_low, NN)
    raw = masks[0] * product[:fields]
    for s in range(1, 8):
        raw += masks[s] * product[s * fields : (s + 1) * fields]

    def mix(matrix, values):
        return lax.dot_general(
            matrix, values, NN, precision=HIGHEST, preferred_element_type=jnp.float32
        )

    eigen = degree * (degree + 1.0) * (1.0 / (waves * waves))
    projected = mix(modes_ref[...], raw) / (1.0 + rates_ref[...] * eigen)
    spectral = mix(back_ref[...], projected)
    spec_ref[...] = spectral
    parts = jnp.concatenate([masks[s] * spectral for s in range(8)], axis=0)
    sums = dot_split(*both_halves(parts), leg_high, leg_low, NT)
    out_ref[here] += sums[:rows]
    out_ref[there] += sums[rows:]


def smem():
    return pl.BlockSpec(memory_space=pltpu.SMEM)


def vmem():
    return pl.BlockSpec(memory_space=pltpu.VMEM)


def exchange(blocks, axes):
    shape = blocks.shape
    count = math.prod(shape[1:])
    dense = (shape[0], count // 128, 128) if count % 128 == 0 else (shape[0], 1, count)
    sent = lax.all_to_all(blocks.reshape(dense), axes, split_axis=0, concat_axis=0, tiled=True)
    return sent.reshape(shape)


def body(
    n_wave, n_lev, grid, row_points, lat_of_slot, pair_low, legendre, lat_weight, vert_modes, vert_back, vert_rates
):
    levels = grid.shape[0]
    ld = levels // n_lev
    waves = lat_of_slot.shape[0]
    half = waves // 2
    points = grid.shape[2] * n_wave
    lats = half // n_wave
    pair_count = legendre.shape[1] // (waves + 1)
    used = pair_count * (waves + 1)
    modes_pad = (used + 127) // 128 * 128
    span = -(-pair_count // n_lev)
    outer = -(-points // (INNER * 8)) * 8
    vectors = 2 * ld
    fields = 2 * levels
    devices = n_wave * n_lev
    wave_index = lax.axis_index("wave")
    lev_index = lax.axis_index("lev")

    low_blocks = pair_low.reshape(n_wave, pair_count)
    order = jnp.stack([low_blocks, waves - 1 - low_blocks], axis=2)
    order = jnp.pad(
        order, ((0, 0), (0, n_lev * span - pair_count), (0, 0)), constant_values=points
    )
    order = order.reshape(1, devices * span * 2).astype(jnp.float32)
    columns = order.shape[1]
    my_points = lax.dynamic_slice_in_dim(row_points, wave_index * lats, lats).astype(jnp.float32)
    facts = jnp.stack([my_points, 1.0 / my_points, lax.rsqrt(my_points)])

    lat_idx = jnp.arange(half, dtype=jnp.int32)[:, None]
    north = (lat_of_slot[None, :] == lat_idx).astype(jnp.float32)
    south = (lat_of_slot[None, :] == waves - 1 - lat_idx).astype(jnp.float32)
    unfold = jnp.stack([north + south, north - south], axis=1)
    fold = (unfold * lat_weight[:, None, None]).reshape(waves, waves)
    unfold = unfold.reshape(waves, waves)

    whole = lax.all_to_all(grid, "lev", split_axis=0, concat_axis=1, tiled=True)
    folded = jnp.einsum("xs,lsj->lxj", fold, whole, precision=HIGHEST)
    rows_in = lax.all_to_all(folded, "wave", split_axis=1, concat_axis=2, tiled=True)
    rows_in = rows_in.reshape(ld, lats, 2, points).transpose(1, 2, 0, 3)
    rows_in = jnp.pad(rows_in, ((0, 0), (0, 0), (0, 0), (0, outer * INNER - points)))
    rows_in = rows_in.reshape(lats, vectors * outer, INNER)

    params = pltpu.CompilerParams(vmem_limit_bytes=48 * 1024 * 1024)
    fourier = pl.pallas_call(
        functools.partial(forward_kernel, vectors, outer),
        out_shape=jax.ShapeDtypeStruct((lats, 2 * vectors, columns), jnp.float32),
        in_specs=[smem(), vmem(), vmem()],
        out_specs=vmem(),
        compiler_params=params,
        name="forward_rows",
    )(facts, rows_in, order)

    fourier = fourier.reshape(lats, 2, ld, 2, devices, 2 * span).transpose(4, 5, 1, 2, 3, 0)
    arrived = exchange(fourier, BOTH).reshape(n_wave, n_lev, span, 2, 2, ld, 2, lats)
    four = arrived.transpose(2, 3, 4, 1, 5, 6, 0, 7).reshape(span, 4 * fields, half)

    starts = [min(l * span * (waves + 1), used - 1) // WIDTH for l in range(n_lev)]
    stops = [-(-min((l + 1) * span * (waves + 1), used) // WIDTH) for l in range(n_lev)]
    steps = max(1, max(b - a for a, b in zip(starts, stops)))
    final_block = (used - 1) // WIDTH
    start = jnp.minimum(lev_index * span * (waves + 1), used - 1) // WIDTH
    place = jnp.stack([start, lev_index * span]).astype(jnp.int32)
    my_low = lax.dynamic_slice_in_dim(pair_low, wave_index * pair_count, pair_count)
    pair_eye = jnp.eye(2, dtype=jnp.float32)
    grow = lambda m: (m[:, None, :, None] * pair_eye[None, :, None, :]).reshape(fields, fields)
    rates = jnp.repeat(vert_rates, 2)[:, None]
    fixed = lambda *shape: pl.BlockSpec(shape, lambda t, *_: (0,) * len(shape))
    spec, back = pl.pallas_call(
        functools.partial(legendre_kernel, waves, used, span),
        out_shape=(
            jax.ShapeDtypeStruct((fields, steps * WIDTH), jnp.float32),
            jax.ShapeDtypeStruct((span, 4 * fields, half), jnp.float32),
        ),
        grid_spec=pltpu.PrefetchScalarGridSpec(
            num_scalar_prefetch=2,
            grid=(steps,),
            in_specs=[
                fixed(span, 4 * fields, half),
                pl.BlockSpec(
                    (half, WIDTH), lambda t, p, _: (0, jnp.minimum(p[0] + t, final_block))
                ),
                fixed(fields, fields),
                fixed(fields, fields),
                fixed(fields, 1),
            ],
            out_specs=[
                pl.BlockSpec((fields, WIDTH), lambda t, *_: (0, t)),
                fixed(span, 4 * fields, half),
            ],
        ),
        compiler_params=params,
        name="legendre_both",
    )(place, my_low, four, legendre, grow(vert_modes), grow(vert_back), rates)

    pieces = lax.all_to_all(
        spec.reshape(n_lev, fields // n_lev, steps * WIDTH), "lev", split_axis=0, concat_axis=0, tiled=True
    )
    full = (final_block + 1 + steps) * WIDTH
    spectral = sum(
        jnp.pad(pieces[l], ((0, 0), (starts[l] * WIDTH, full - (starts[l] + steps) * WIDTH)))
        for l in range(n_lev)
    )
    spectral = spectral[:, :modes_pad].reshape(ld, 2, modes_pad)

    back = back.reshape(span, 2, 2, n_lev, ld, 2, n_wave, lats).transpose(6, 3, 0, 1, 2, 4, 5, 7)
    returned = exchange(back.reshape(devices, 2 * span, 2, ld, 2, lats), BOTH)
    returned = returned.transpose(5, 2, 3, 4, 0, 1).reshape(lats, 2 * vectors, columns)
    values = pl.pallas_call(
        functools.partial(inverse_kernel, vectors, outer, 1.0 / math.sqrt(waves)),
        out_shape=jax.ShapeDtypeStruct((lats, vectors * outer, INNER), jnp.float32),
        in_specs=[smem(), vmem(), vmem()],
        out_specs=vmem(),
        compiler_params=params,
        name="inverse_rows",
    )(facts, returned, order)
    values = values.reshape(lats, 2, ld, outer * INNER)[..., :points]
    values = values.transpose(2, 0, 1, 3).reshape(ld, 2 * lats, points)
    values = lax.all_to_all(values, "wave", split_axis=2, concat_axis=1, tiled=True)
    slots = jnp.einsum("xs,lxj->lsj", unfold, values, precision=HIGHEST)
    grid_out = lax.all_to_all(slots, "lev", split_axis=1, concat_axis=0, tiled=True)
    return spectral, grid_out


def solution(mesh):
    placed = (P(None, "lev", "wave"), P(), P(), P(), P(None, "wave"), P(), P(), P(), P())
    return jax.shard_map(
        functools.partial(body, mesh.shape["wave"], mesh.shape["lev"]),
        mesh=mesh,
        in_specs=placed,
        out_specs=(P("lev", None, "wave"), P(None, "lev", "wave")),
        check_vma=False,
    )
```

time: 2480 us -> 214 us (0.09)
  local copies, waits for them, and re-layouts: 1280 us -> 44.5 us
  matrix products: 665 us -> 5.17 us
  other arithmetic: 417 us -> 3.52 us
  Pallas kernels: 0 us -> 53.1 us
  waiting for transfers between devices: 30.9 us -> 77.7 us
  blocking collectives: 43.6 us -> 0 us
    gather x22 -> x0, local copies, waits for them, and re-layouts: 1060 us -> none  [the longest x4 429 us: body(): leg_sorted = jnp.take_along_axis(legendre_cols, order[None], axis=2)]
    dot_general x14 -> x2, matrix products: 665 us -> 5.17 us  [the longest x1 3.71 us: body(): folded = jnp.einsum('xs,lsj->lxj', fold, whole, precision=HIGHEST)]
    dot_general x2 -> x0, other arithmetic: 318 us -> none  [the longest x1 166 us: inverse_dft(): jnp.einsum('vsom,sjm->vsoj', turned_real, cos_in, precision=PRECISE)]
    reshape x17 -> x10, local copies, waits for them, and re-layouts: 95.8 us -> 18.6 us  [the longest x1 4.36 us: exchange(): return sent.reshape(shape)]
    pallas_call x0 -> x3, Pallas kernels: none -> 53.1 us  [the longest x1 20.1 us: body(): pl.pallas_call(functools.partial(inverse_kernel, vectors, outer, 1.0 / ma...]
    all_to_all x4 -> x7, waiting for transfers between devices: 30.9 us -> 77.7 us  [the longest x2 29.5 us: exchange(): lax.all_to_all(blocks.reshape(dense), axes, split_axis=0, concat_axis=0,...]
    pad x3 -> x1, local copies, waits for them, and re-layouts: 38.2 us -> 0.16 us  [body(): jnp.pad(rows_in, ((0, 0), (0, 0), (0, 0), (0, outer * INNER - points)))]
    sort x2 -> x0, other arithmetic: 35.2 us -> none  [the longest x1 17.9 us: column_order(): order = jnp.argsort(score, axis=1)]
  transfers between devices with their start and end apart: 4 -> 7, of which waited for: 2 -> 6; matrix products, arithmetic and copies ran while one was open for 29% -> 10% of each run, Pallas kernels for 0% -> 9%
where the time goes in v1:
time: 214 us; the launch traced here: 213 us
  waiting for transfers between devices  77.7 us (36%)
  Pallas kernels  53.1 us (25%)
  local copies, waits for them, and re-layouts  44.5 us (21%)
  starting transfers between devices  28 us (13%)
  matrix products  5.17 us (2%)
  other arithmetic  3.52 us (2%)
    all_to_all x2, waiting for transfers between devices, exchange(): lax.all_to_all(blocks.reshape(dense), axes, split_axis=0, concat_axis=0,...  29.5 us
    pallas_call x1, Pallas kernels, body(): pl.pallas_call(functools.partial(inverse_kernel, vectors, outer, 1.0 / ma...  20.1 us
    all_to_all x1, waiting for transfers between devices, body(): lax.all_to_all(values, 'wave', split_axis=2, concat_axis=1, tiled=True)  18.6 us
    pallas_call x1, Pallas kernels, body(): pl.pallas_call(functools.partial(forward_kernel, vectors, outer), out_sha...  17.7 us
    pallas_call x1, Pallas kernels, body(): pl.pallas_call(functools.partial(legendre_kernel, waves, used, span), out...  15.3 us
    all_to_all x1, waiting for transfers between devices, body(): lax.all_to_all(folded, 'wave', split_axis=1, concat_axis=2, tiled=True)  15.2 us
    all_to_all x1, waiting for transfers between devices, body(): lax.all_to_all(slots, 'lev', split_axis=1, concat_axis=0, tiled=True)  9.51 us
    all_to_all x1, starting transfers between devices, body(): lax.all_to_all(folded, 'wave', split_axis=1, concat_axis=2, tiled=True)  6.64 us
  transfers between devices with their start and end apart: 7, of which 6 were waited for; matrix products, arithmetic and copies ran while one was open for 10% of the time, Pallas kernels for 9%

profile of v1, /device:TPU:0, one launch (start us, length us, event | category | flops | bytes accessed | tf_op | source)
XLA Modules:
  0.0 212.9 jit_solution(4902136936568174121)
XLA Ops:
  0.6 4.2 %all-to-all-start = ((f32[4,160,168]{2,1,0:T(8,128)}), f32[4,160,168]{2,1,0:T(8,128)}, u32[]{:S(2)}, u32[]{:S(2)}) async-start(f32[4,160,168]{2,1,0:T(8,128)} %param.9), calls=%async_computation | async-start | bytes 1310720 | tf_op jit(solution)/shard_map/all_to_all | solution.py:239
  4.9 0.9 convert_add_fusion
  6.0 2.5 %copy.77 = f32[320,2,640]{2,1,0:T(2,128)} copy(f32[320,2,640]{2,0,1:T(8,128)S(1)} %get-tuple-element.21) | data formatting | bytes 3276800 | tf_op jit(solution)/shard_map/mul | solution.py:236
  8.5 2.4 %mul.68 = f32[640,640]{1,0:T(8,128)S(1)} reshape(f32[320,2,640]{2,1,0:T(2,128)} %copy.77) | data formatting | bytes 3276800 | tf_op jit(solution)/shard_map/mul | solution.py:236
  10.9 4.9 %all-to-all-done = f32[4,160,168]{2,1,0:T(8,128)} async-done(((f32[4,160,168]{2,1,0:T(8,128)}), f32[4,160,168]{2,1,0:T(8,128)}, u32[]{:S(2)}, u32[]{:S(2)}) %all-to-all-start) | async-done | bytes 430112 | tf_op jit(solution)/shard_map/all_to_all | solution.py:239
  15.8 3.7 %convolution_bitcast_fusion.1 = f32[1,640,168]{1,2,0:T(8,128)} fusion(f32[640,640]{1,0:T(8,128)S(1)} %mul.68, f32[640,168]{1,0:T(8,128)} %bitcast.5), kind=kOutput, calls=%fused_computation.3 | convolution fusion | flops 825753600 | bytes 2498560 | tf_op jit(solution)/shard_map/xs,lsj->lxj/dot_general | solution.py:240
  19.5 2.1 copy.78
  21.5 6.6 %all-to-all-start.1 = ((f32[1,640,168]{2,0,1:T(1,128)}), f32[1,640,168]{2,0,1:T(1,128)S(1)}, u32[]{:S(2)}, u32[]{:S(2)}) async-start(f32[1,640,168]{2,0,1:T(1,128)} %copy.78), calls=%async_computation.1 | async-start | bytes 1310720 | tf_op jit(solution)/shard_map/all_to_all | solution.py:241
  28.5 0.8 convert_bitcast_fusion
  29.3 0.8 divide_bitcast_fusion
  30.1 15.2 %all-to-all-done.1 = f32[1,640,168]{2,0,1:T(1,128)S(1)} async-done(((f32[1,640,168]{2,0,1:T(1,128)}), f32[1,640,168]{2,0,1:T(1,128)S(1)}, u32[]{:S(2)}, u32[]{:S(2)}) %all-to-all-start.1) | async-done | bytes 430112 | tf_op jit(solution)/shard_map/all_to_all | solution.py:241
  45.3 0.9 copy.79
  46.5 0.4 copy.80
  46.9 0.7 transpose_reshape.3
  47.8 0.6 reshape.266.x_ref
  48.3 17.7 %forward_rows.1 = f32[40,4,640]{2,1,0:T(4,128)S(1)} custom-call(f32[3,40]{1,0:T(4,128)S(1)} %pad_maximum_fusion.1.facts, f32[40,48,64]{2,1,0:T(8,128)S(1)} %reshape.266.x_ref, f32[1,640]{1,0:T(1,128)S(1)} %convert_element_type.59.wave_ref), custom_call_target="tpu_custom_call" | custom-call | tf_op jit(solution)/shard_map/forward_rows/pallas_call | solution.py:247
  66.1 1.5 copy.82
  67.6 4.2 %reshape.268 = f32[32,25,128]{2,1,0:T(8,128)} reshape(f32[32,20,2,1,2,40]{5,4,2,1,0,3:T(2,128)} %bitcast.66) | data formatting | bytes 819200 | tf_op jit(solution)/shard_map/reshape | solution.py:198
  71.7 3.5 %all-to-all-start.2 = ((f32[32,25,128]{2,1,0:T(8,128)}), f32[32,25,128]{2,1,0:T(8,128)}, u32[]{:S(2)}, u32[]{:S(2)}) async-start(f32[32,25,128]{2,1,0:T(8,128)} %reshape.268), calls=%async_computation.2 | async-start | bytes 1048576 | tf_op jit(solution)/shard_map/all_to_all | solution.py:198
  75.8 14.8 %all-to-all-done.2 = f32[32,25,128]{2,1,0:T(8,128)} async-done(((f32[32,25,128]{2,1,0:T(8,128)}), f32[32,25,128]{2,1,0:T(8,128)}, u32[]{:S(2)}, u32[]{:S(2)}) %all-to-all-start.2) | async-done | bytes 409632 | tf_op jit(solution)/shard_map/all_to_all | solution.py:198
  90.6 3.3 %reshape_reshape.6 = f32[8,4,10,2,2,1,2,40]{7,6,4,3,2,1,0,5:T(2,128)S(1)} reshape(f32[32,25,128]{2,1,0:T(8,128)} %all-to-all-done.2) | data formatting | bytes 819200 | tf_op jit(solution)/shard_map/reshape;reshape | solution.py:257
  93.9 1.8 copy.83
  95.7 1.7 reshape.269.four_ref
  97.4 15.3 %legendre_both.1 = (f32[8,7168]{1,0:T(8,128)S(1)}, f32[10,32,320]{2,1,0:T(8,128)S(1)}) custom-call(s32[2]{0:T(128)S(1)} %pad_add_fusion.3.place, s32[40]{0:T(128)S(1)} %dynamic_slice.6.low, f32[10,32,320]{2,1,0:T(8,128)S(1)} %reshape.269.four_ref, f32[320,25640]{1,0:T(8,128)} %leg_ref.1, f32[8,8]{1,0:T(8,128)S(1)} %mul.72.modes_ref, ...), custom_call_target="tpu_custom_call" | custom-call | tf_op jit(solution)/shard_map/legendre_both/pallas_call | solution.py:271
  112.7 1.6 reshape.272
  114.3 2.0 copy.99
  116.3 2.8 %reshape_reshape.7 = f32[32,25,128]{2,1,0:T(8,128)} reshape(f32[8,4,10,2,2,1,2,40]{7,6,4,3,2,1,0,5:T(2,128)S(1)} %bitcast.68) | data formatting | bytes 819200 | tf_op jit(solution)/shard_map/reshape;reshape | solution.py:198
  119.1 3.0 %all-to-all-start.4 = ((f32[32,25,128]{2,1,0:T(8,128)}), f32[32,25,128]{2,1,0:T(8,128)S(1)}, u32[]{:S(2)}, u32[]{:S(2)}) async-start(f32[32,25,128]{2,1,0:T(8,128)} %reshape_reshape.7), calls=%async_computation.4 | async-start | bytes 1048576 | tf_op jit(solution)/shard_map/all_to_all | solution.py:198
  122.1 0.8 reshape.270
  122.9 14.7 %all-to-all-done.4 = f32[32,25,128]{2,1,0:T(8,128)S(1)} async-done(((f32[32,25,128]{2,1,0:T(8,128)}), f32[32,25,128]{2,1,0:T(8,128)S(1)}, u32[]{:S(2)}, u32[]{:S(2)}) %all-to-all-start.4) | async-done | bytes 409632 | tf_op jit(solution)/shard_map/all_to_all | solution.py:198
  137.6 3.6 %all-to-all-start.3 = ((f32[4,2,7168]{2,1,0:T(2,128)}), f32[4,2,7168]{2,1,0:T(2,128)S(1)}, u32[]{:S(2)}, u32[]{:S(2)}) async-start(f32[4,2,7168]{2,1,0:T(2,128)} %reshape.270), calls=%async_computation.3 | async-start | bytes 458752 | tf_op jit(solution)/shard_map/all_to_all | solution.py:298
  141.2 1.3 copy.91
  142.5 1.1 reshape.277
  143.6 4.4 %reshape.273 = f32[32,20,2,1,2,40]{5,4,2,1,0,3:T(2,128)} reshape(f32[32,25,128]{2,1,0:T(8,128)} %copy-done) | data formatting | bytes 819200 | tf_op jit(solution)/shard_map/reshape | solution.py:199
  148.0 1.7 copy.86.f_ref
  149.7 20.1 %inverse_rows.1 = f32[40,48,64]{2,1,0:T(8,128)S(1)} custom-call(f32[3,40]{1,0:T(4,128)S(1)} %pad_maximum_fusion.1.facts, f32[40,4,640]{2,1,0:T(4,128)S(1)} %copy.86.f_ref, f32[1,640]{1,0:T(1,128)S(1)} %convert_element_type.59.wave_ref), custom_call_target="tpu_custom_call" | custom-call | tf_op jit(solution)/shard_map/inverse_rows/pallas_call | solution.py:311
  169.8 0.6 reshape.278
  170.5 1.9 copy.88
  172.4 3.5 %all-to-all-start.5 = ((f32[1,80,1344]{1,0,2:T(1,128)}), f32[1,80,1344]{1,0,2:T(1,128)S(1)}, u32[]{:S(2)}, u32[]{:S(2)}) async-start(f32[1,80,1344]{1,0,2:T(1,128)} %copy.88), calls=%async_computation.5 | async-start | bytes 1376256 | tf_op jit(solution)/shard_map/all_to_all | solution.py:321
  176.0 18.6 %all-to-all-done.5 = f32[1,80,1344]{1,0,2:T(1,128)S(1)} async-done(((f32[1,80,1344]{1,0,2:T(1,128)}), f32[1,80,1344]{1,0,2:T(1,128)S(1)}, u32[]{:S(2)}, u32[]{:S(2)}) %all-to-all-start.5) | async-done | bytes 430112 | tf_op jit(solution)/shard_map/all_to_all | solution.py:321
  194.6 0.4 copy.95
  195.0 0.4 copy.90
  195.7 1.5 convolution_bitcast_fusion
  197.2 1.2 copy.92
  198.3 3.5 %all-to-all-start.6 = ((f32[1,640,168]{2,0,1:T(1,128)}), f32[1,640,168]{2,0,1:T(1,128)S(1)}, u32[]{:S(2)}, u32[]{:S(2)}) async-start(f32[1,640,168]{2,0,1:T(1,128)} %copy.92), calls=%async_computation.6 | async-start | bytes 1310720 | tf_op jit(solution)/shard_map/all_to_all | solution.py:323
  201.8 0.7 fusion
  202.5 9.5 %all-to-all-done.6 = f32[1,640,168]{2,0,1:T(1,128)S(1)} async-done(((f32[1,640,168]{2,0,1:T(1,128)}), f32[1,640,168]{2,0,1:T(1,128)S(1)}, u32[]{:S(2)}, u32[]{:S(2)}) %all-to-all-start.6) | async-done | bytes 430112 | tf_op jit(solution)/shard_map/all_to_all | solution.py:323
  212.1 0.9 copy.97
  (34 shorter events, 2.0 us)
Async XLA Ops:
  0.6 5.2 %copy-start.1 = (f32[320]{0:T(512)S(1)}, f32[320]{0:T(512)}, u32[]{:S(2)}) copy-start(f32[320]{0:T(512)} %param.14) | copy-start | bytes 3844
  0.6 15.1 %all-to-all-start = ((f32[4,160,168]{2,1,0:T(8,128)}), f32[4,160,168]{2,1,0:T(8,128)}, u32[]{:S(2)}, u32[]{:S(2)}) async-start(f32[4,160,168]{2,1,0:T(8,128)} %param.9), calls=%async_computation | async-start | bytes 1310720 | tf_op jit(solution)/shard_map/all_to_all | solution.py:239
  19.5 8.7 %copy-start.2 = (s32[320]{0:T(512)S(1)}, s32[320]{0:T(512)}, u32[]{:S(2)}) copy-start(s32[320]{0:T(512)} %param.12) | copy-start | bytes 3844
  21.5 23.7 %all-to-all-start.1 = ((f32[1,640,168]{2,0,1:T(1,128)}), f32[1,640,168]{2,0,1:T(1,128)S(1)}, u32[]{:S(2)}, u32[]{:S(2)}) async-start(f32[1,640,168]{2,0,1:T(1,128)} %copy.78), calls=%async_computation.1 | async-start | bytes 1310720 | tf_op jit(solution)/shard_map/all_to_all | solution.py:241
  67.6 7.8 %copy-start.3 = (f32[4,4]{1,0:T(4,128)S(1)}, f32[4,4]{1,0:T(4,128)}, u32[]{:S(2)}) copy-start(f32[4,4]{1,0:T(4,128)} %param.16) | copy-start | bytes 196
  67.6 7.8 %copy-start.4 = (f32[4,4]{1,0:T(4,128)S(1)}, f32[4,4]{1,0:T(4,128)}, u32[]{:S(2)}) copy-start(f32[4,4]{1,0:T(4,128)} %param.15) | copy-start | bytes 196
  67.6 8.0 %copy-start.5 = (f32[4]{0:T(128)S(1)}, f32[4]{0:T(128)}, u32[]{:S(2)}) copy-start(f32[4]{0:T(128)} %param.17) | copy-start | bytes 52
  71.7 18.9 %all-to-all-start.2 = ((f32[32,25,128]{2,1,0:T(8,128)}), f32[32,25,128]{2,1,0:T(8,128)}, u32[]{:S(2)}, u32[]{:S(2)}) async-start(f32[32,25,128]{2,1,0:T(8,128)} %reshape.268), calls=%async_computation.2 | async-start | bytes 1048576 | tf_op jit(solution)/shard_map/all_to_all | solution.py:198
  119.1 18.5 %all-to-all-start.4 = ((f32[32,25,128]{2,1,0:T(8,128)}), f32[32,25,128]{2,1,0:T(8,128)S(1)}, u32[]{:S(2)}, u32[]{:S(2)}) async-start(f32[32,25,128]{2,1,0:T(8,128)} %reshape_reshape.7), calls=%async_computation.4 | async-start | bytes 1048576 | tf_op jit(solution)/shard_map/all_to_all | solution.py:198
  137.6 3.6 %copy-start = (f32[32,25,128]{2,1,0:T(8,128)}, f32[32,25,128]{2,1,0:T(8,128)S(1)}, u32[]{:S(2)}) copy-start(f32[32,25,128]{2,1,0:T(8,128)S(1)} %all-to-all-done.4) | copy-start | bytes 1228804
  137.6 34.8 %all-to-all-start.3 = ((f32[4,2,7168]{2,1,0:T(2,128)}), f32[4,2,7168]{2,1,0:T(2,128)S(1)}, u32[]{:S(2)}, u32[]{:S(2)}) async-start(f32[4,2,7168]{2,1,0:T(2,128)} %reshape.270), calls=%async_computation.3 | async-start | bytes 458752 | tf_op jit(solution)/shard_map/all_to_all | solution.py:298
  172.4 22.2 %all-to-all-start.5 = ((f32[1,80,1344]{1,0,2:T(1,128)}), f32[1,80,1344]{1,0,2:T(1,128)S(1)}, u32[]{:S(2)}, u32[]{:S(2)}) async-start(f32[1,80,1344]{1,0,2:T(1,128)} %copy.88), calls=%async_computation.5 | async-start | bytes 1376256 | tf_op jit(solution)/shard_map/all_to_all | solution.py:321
  198.3 13.7 %all-to-all-start.6 = ((f32[1,640,168]{2,0,1:T(1,128)}), f32[1,640,168]{2,0,1:T(1,128)S(1)}, u32[]{:S(2)}, u32[]{:S(2)}) async-start(f32[1,640,168]{2,0,1:T(1,128)} %copy.92), calls=%async_computation.6 | async-start | bytes 1310720 | tf_op jit(solution)/shard_map/all_to_all | solution.py:323

commit v2 on v1

--- a/solution.py
+++ b/solution.py
@@ -12,7 +12,7 @@
 HIGHEST = lax.Precision.HIGHEST
 BOTH = ("wave", "lev")
 INNER = 64
-WIDTH = 512
+WIDTH = 640
 NN = (((1,), (0,)), ((), ()))
 NT = (((1,), (1,)), ((), ()))
 
@@ -79,14 +79,39 @@
     return (position.astype(jnp.float32) < length).astype(jnp.float32)
 
 
+def angle_sums(cos_base, sin_base, cos_step, sin_step):
+    cos_rows, sin_rows = [], []
+    for k in range(cos_step.shape[0]):
+        c, s = cos_step[k : k + 1], sin_step[k : k + 1]
+        cos_rows.append(cos_base * c - sin_base * s)
+        sin_rows.append(sin_base * c + cos_base * s)
+    return jnp.concatenate(cos_rows, axis=0), jnp.concatenate(sin_rows, axis=0)
+
+
 def tables(wave, length, inverse, outer):
-    inner_idx = row_iota(INNER).astype(jnp.float32)
-    outer_idx = (row_iota(outer) * INNER).astype(jnp.float32)
-    return turn(inner_idx * wave, length, inverse) + turn(outer_idx * wave, length, inverse)
+    row = row_iota(32)
+    scale = jnp.where(row < 16, jnp.where(row < 8, 1, 8), jnp.where(row < 24, 64, 512))
+    multiple = ((row & 7) * scale).astype(jnp.float32)
+    c, s = turn(multiple * wave, length, inverse)
+    top = 24 + outer // 8
+    return angle_sums(c[:8], s[:8], c[8:16], s[8:16]) + angle_sums(
+        c[16:24], s[16:24], c[24:top], s[24:top]
+    )
+
+
+def each_row(rows, one):
+    together = 2 if rows % 2 == 0 else 1
+
+    def some(step, carry):
+        for k in range(together):
+            one(step * together + k)
+        return carry
+
+    lax.fori_loop(0, rows // together, some, 0)
 
 
 def forward_kernel(vectors, outer, facts, x_ref, wave_ref, out_ref):
-    def one(r, carry):
+    def one(r):
         length, inverse, norm = facts[0, r], facts[1, r], facts[2, r]
         wave = wave_ref[...]
         cos_in, sin_in, cos_out, sin_out = tables(wave, length, inverse, outer)
@@ -101,13 +126,12 @@
             rows.append(jnp.sum(p * cos_out - q * sin_out, axis=0, keepdims=True) * keep)
             rows.append(jnp.sum(q * cos_out + p * sin_out, axis=0, keepdims=True) * -keep)
         out_ref[r] = jnp.concatenate(rows, axis=0)
-        return carry
-
-    lax.fori_loop(0, x_ref.shape[0], one, 0)
+
+    each_row(x_ref.shape[0], one)
 
 
 def inverse_kernel(vectors, outer, scale, facts, f_ref, wave_ref, out_ref):
-    def one(r, carry):
+    def one(r):
         length, inverse, norm = facts[0, r], facts[1, r], facts[2, r]
         wave = wave_ref[...]
         cos_in, sin_in, cos_out, sin_out = tables(wave, length, inverse, outer)
@@ -122,9 +146,8 @@
         values = dot_split(*both_halves(jnp.concatenate(real, axis=0)), *halves(cos_in), NT)
         values += dot_split(*both_halves(jnp.concatenate(imaginary, axis=0)), *halves(sin_in), NT)
         out_ref[r] = values * live_mask(length, vectors, outer)
-        return carry
-
-    lax.fori_loop(0, f_ref.shape[0], one, 0)
+
+    each_row(f_ref.shape[0], one)
 
 
 def legendre_kernel(
@@ -228,34 +251,46 @@
     columns = order.shape[1]
     my_points = lax.dynamic_slice_in_dim(row_points, wave_index * lats, lats).astype(jnp.float32)
     facts = jnp.stack([my_points, 1.0 / my_points, lax.rsqrt(my_points)])
-
-    lat_idx = jnp.arange(half, dtype=jnp.int32)[:, None]
+    parts = 2 if lats % 2 == 0 else 1
+    some = lats // parts
+    facts = [facts[:, k * some : (k + 1) * some] for k in range(parts)]
+
+    lat_idx = jnp.arange(half, dtype=jnp.int32).reshape(n_wave, parts, some).transpose(1, 0, 2)
+    lat_idx = lat_idx.reshape(half, 1)
     north = (lat_of_slot[None, :] == lat_idx).astype(jnp.float32)
     south = (lat_of_slot[None, :] == waves - 1 - lat_idx).astype(jnp.float32)
     unfold = jnp.stack([north + south, north - south], axis=1)
-    fold = (unfold * lat_weight[:, None, None]).reshape(waves, waves)
+    weight = lat_weight.reshape(n_wave, parts, some).transpose(1, 0, 2).reshape(half, 1, 1)
+    fold = (unfold * weight).reshape(parts, waves // parts, waves)
     unfold = unfold.reshape(waves, waves)
 
+    params = pltpu.CompilerParams(vmem_limit_bytes=48 * 1024 * 1024)
+    cost = pl.CostEstimate(flops=some * 2 * 10**8, bytes_accessed=2 * 10**6, transcendentals=0)
     whole = lax.all_to_all(grid, "lev", split_axis=0, concat_axis=1, tiled=True)
-    folded = jnp.einsum("xs,lsj->lxj", fold, whole, precision=HIGHEST)
-    rows_in = lax.all_to_all(folded, "wave", split_axis=1, concat_axis=2, tiled=True)
-    rows_in = rows_in.reshape(ld, lats, 2, points).transpose(1, 2, 0, 3)
-    rows_in = jnp.pad(rows_in, ((0, 0), (0, 0), (0, 0), (0, outer * INNER - points)))
-    rows_in = rows_in.reshape(lats, vectors * outer, INNER)
-
-    params = pltpu.CompilerParams(vmem_limit_bytes=48 * 1024 * 1024)
-    fourier = pl.pallas_call(
-        functools.partial(forward_kernel, vectors, outer),
-        out_shape=jax.ShapeDtypeStruct((lats, 2 * vectors, columns), jnp.float32),
-        in_specs=[smem(), vmem(), vmem()],
-        out_specs=vmem(),
-        compiler_params=params,
-        name="forward_rows",
-    )(facts, rows_in, order)
-
-    fourier = fourier.reshape(lats, 2, ld, 2, devices, 2 * span).transpose(4, 5, 1, 2, 3, 0)
-    arrived = exchange(fourier, BOTH).reshape(n_wave, n_lev, span, 2, 2, ld, 2, lats)
-    four = arrived.transpose(2, 3, 4, 1, 5, 6, 0, 7).reshape(span, 4 * fields, half)
+    pieces = []
+    for k in range(parts):
+        folded = jnp.einsum("xs,lsj->lxj", fold[k], whole, precision=HIGHEST)
+        pieces.append(lax.all_to_all(folded, "wave", split_axis=1, concat_axis=2, tiled=True))
+    arrived = []
+    for k in range(parts):
+        rows_in = pieces[k].reshape(ld, some, 2, points).transpose(1, 2, 0, 3)
+        rows_in = jnp.pad(rows_in, ((0, 0), (0, 0), (0, 0), (0, outer * INNER - points)))
+        rows_in = rows_in.reshape(some, vectors * outer, INNER)
+        fourier = pl.pallas_call(
+            functools.partial(forward_kernel, vectors, outer),
+            out_shape=jax.ShapeDtypeStruct((some, 2 * vectors, columns), jnp.float32),
+            in_specs=[smem(), vmem(), vmem()],
+            out_specs=vmem(),
+            compiler_params=params,
+            cost_estimate=cost,
+            name="forward_rows",
+        )(facts[k], rows_in, order)
+        fourier = fourier.reshape(some, 2, ld, 2, devices, 2 * span).transpose(4, 5, 1, 2, 3, 0)
+        arrived.append(
+            exchange(fourier, BOTH).reshape(n_wave, n_lev, span, 2, 2, ld, 2, some)
+        )
+    four = jnp.stack(arrived, axis=7).transpose(2, 3, 4, 1, 5, 6, 0, 7, 8)
+    four = four.reshape(span, 4 * fields, half)
 
     starts = [min(l * span * (waves + 1), used - 1) // WIDTH for l in range(n_lev)]
     stops = [-(-min((l + 1) * span * (waves + 1), used) // WIDTH) for l in range(n_lev)]
@@ -295,6 +330,11 @@
         name="legendre_both",
     )(place, my_low, four, legendre, grow(vert_modes), grow(vert_back), rates)
 
+    back = back.reshape(span, 2, 2, n_lev, ld, 2, n_wave, parts, some)
+    back = back.transpose(7, 6, 3, 0, 1, 2, 4, 5, 8)
+    back = back.reshape(parts, devices, 2 * span, 2, ld, 2, some)
+    returned = [exchange(back[k], BOTH) for k in range(parts)]
+
     pieces = lax.all_to_all(
         spec.reshape(n_lev, fields // n_lev, steps * WIDTH), "lev", split_axis=0, concat_axis=0, tiled=True
     )
@@ -305,20 +345,22 @@
     )
     spectral = spectral[:, :modes_pad].reshape(ld, 2, modes_pad)
 
-    back = back.reshape(span, 2, 2, n_lev, ld, 2, n_wave, lats).transpose(6, 3, 0, 1, 2, 4, 5, 7)
-    returned = exchange(back.reshape(devices, 2 * span, 2, ld, 2, lats), BOTH)
-    returned = returned.transpose(5, 2, 3, 4, 0, 1).reshape(lats, 2 * vectors, columns)
-    values = pl.pallas_call(
-        functools.partial(inverse_kernel, vectors, outer, 1.0 / math.sqrt(waves)),
-        out_shape=jax.ShapeDtypeStruct((lats, vectors * outer, INNER), jnp.float32),
-        in_specs=[smem(), vmem(), vmem()],
-        out_specs=vmem(),
-        compiler_params=params,
-        name="inverse_rows",
-    )(facts, returned, order)
-    values = values.reshape(lats, 2, ld, outer * INNER)[..., :points]
-    values = values.transpose(2, 0, 1, 3).reshape(ld, 2 * lats, points)
-    values = lax.all_to_all(values, "wave", split_axis=2, concat_axis=1, tiled=True)
+    finished = []
+    for k in range(parts):
+        columns_back = returned[k].transpose(5, 2, 3, 4, 0, 1).reshape(some, 2 * vectors, columns)
+        values = pl.pallas_call(
+            functools.partial(inverse_kernel, vectors, outer, 1.0 / math.sqrt(waves)),
+            out_shape=jax.ShapeDtypeStruct((some, vectors * outer, INNER), jnp.float32),
+            in_specs=[smem(), vmem(), vmem()],
+            out_specs=vmem(),
+            compiler_params=params,
+            cost_estimate=cost,
+            name="inverse_rows",
+        )(facts[k], columns_back, order)
+        values = values.reshape(some, 2, ld, outer * INNER)[..., :points]
+        values = values.transpose(2, 0, 1, 3).reshape(ld, 2 * some, points)
+        finished.append(lax.all_to_all(values, "wave", split_axis=2, concat_axis=1, tiled=True))
+    values = jnp.concatenate(finished, axis=1)
     slots = jnp.einsum("xs,lxj->lsj", unfold, values, precision=HIGHEST)
     grid_out = lax.all_to_all(slots, "lev", split_axis=1, concat_axis=0, tiled=True)
     return spectral, grid_out

time: 214 us -> 242 us (1.13); the launches traced: 213 us -> 237 us
  waiting for transfers between devices: 77.7 us -> 36.2 us
  starting transfers between devices: 28 us -> 62.4 us
  local copies, waits for them, and re-layouts: 44.5 us -> 66.7 us
  other arithmetic: 3.52 us -> 25.1 us
  Pallas kernels: 53.1 us -> 40.9 us
    all_to_all x2 -> x4, starting transfers between devices: 6.49 us -> 28.7 us  [exchange(): lax.all_to_all(blocks.reshape(dense), axes, split_axis=0, concat_axis=0,...]
    all_to_all x2 -> x4, waiting for transfers between devices: 29.5 us -> 12.8 us  [exchange(): lax.all_to_all(blocks.reshape(dense), axes, split_axis=0, concat_axis=0,...]
    all_to_all x1 -> x2, waiting for transfers between devices: 18.6 us -> 3.44 us  [body(): lax.all_to_all(values, 'wave', split_axis=2, concat_axis=1, tiled=True)]
    unnamed x0 -> x2, other arithmetic: none -> 12.8 us
    reshape x6 -> x13, local copies, waits for them, and re-layouts: 8.12 us -> 17.2 us  [the longest x2 5.41 us: body(): back = back.reshape(span, 2, 2, n_lev, ld, 2, n_wave, parts, some)]
    all_to_all x1 -> x2, starting transfers between devices: 3.54 us -> 12.4 us  [body(): lax.all_to_all(values, 'wave', split_axis=2, concat_axis=1, tiled=True)]
    all_to_all x1 -> x2, waiting for transfers between devices: 15.2 us -> 7.72 us  [body(): lax.all_to_all(folded, 'wave', split_axis=1, concat_axis=2, tiled=True)]
    all_to_all x0 -> x6, other arithmetic: none -> 6.26 us  [the longest x2 3.3 us: body(): lax.all_to_all(values, 'wave', split_axis=2, concat_axis=1, tiled=True)]
  transfers between devices with their start and end apart: 7 -> 11, of which waited for: 6 -> 6; matrix products, arithmetic and copies ran while one was open for 10% -> 31% of each run, Pallas kernels for 9% -> 12%
where the time goes in v2:
time: 242 us; the launch traced here: 237 us
  local copies, waits for them, and re-layouts  66.7 us (28%)
  starting transfers between devices  62.4 us (26%)
  Pallas kernels  40.9 us (17%)
  waiting for transfers between devices  36.2 us (15%)
  other arithmetic  25.1 us (10%)
  matrix products  4.59 us (2%)
    all_to_all x4, starting transfers between devices, exchange(): lax.all_to_all(blocks.reshape(dense), axes, split_axis=0, concat_axis=0,...  28.7 us
    pallas_call x2, Pallas kernels, body(): pl.pallas_call(functools.partial(inverse_kernel, vectors, outer, 1.0 / ma...  15 us
    pallas_call x1, Pallas kernels, body(): pl.pallas_call(functools.partial(legendre_kernel, waves, used, span), out...  13.5 us
    all_to_all x4, waiting for transfers between devices, exchange(): lax.all_to_all(blocks.reshape(dense), axes, split_axis=0, concat_axis=0,...  12.8 us
    unnamed x2, other arithmetic  12.8 us
    pallas_call x2, Pallas kernels, body(): pl.pallas_call(functools.partial(forward_kernel, vectors, outer), out_sha...  12.4 us
    all_to_all x2, starting transfers between devices, body(): lax.all_to_all(values, 'wave', split_axis=2, concat_axis=1, tiled=True)  12.4 us
    all_to_all x2, starting transfers between devices, body(): lax.all_to_all(folded, 'wave', split_axis=1, concat_axis=2, tiled=True)  10.1 us
  transfers between devices with their start and end apart: 11, of which 6 were waited for; matrix products, arithmetic and copies ran while one was open for 31% of the time, Pallas kernels for 12%

profile of v2, /device:TPU:0, one launch (start us, length us, event | category | flops | bytes accessed | tf_op | source)
XLA Modules:
  0.0 237.4 jit_solution(3080307506048703712)
XLA Ops:
  0.6 4.2 %all-to-all-start = ((f32[4,160,168]{2,1,0:T(8,128)}), f32[4,160,168]{2,1,0:T(8,128)S(1)}, u32[]{:S(2)}, u32[]{:S(2)}) async-start(f32[4,160,168]{2,1,0:T(8,128)} %param.9), calls=%async_computation | async-start | bytes 1310720 | tf_op jit(solution)/shard_map/all_to_all | solution.py:269
  8.3 1.4 pad_maximum_fusion
  12.3 2.8 %all-to-all-done = f32[4,160,168]{2,1,0:T(8,128)S(1)} async-done(((f32[4,160,168]{2,1,0:T(8,128)}), f32[4,160,168]{2,1,0:T(8,128)S(1)}, u32[]{:S(2)}, u32[]{:S(2)}) %all-to-all-start) | async-done | bytes 430112 | tf_op jit(solution)/shard_map/all_to_all | solution.py:269
  15.1 1.5 convolution_bitcast_fusion.1
  17.5 6.5 %all-to-all-start.3 = ((f32[1,320,168]{2,0,1:T(1,128)}), f32[1,320,168]{2,0,1:T(1,128)S(1)}, u32[]{:S(2)}, u32[]{:S(2)}) async-start(f32[1,320,168]{2,0,1:T(1,128)} %copy.132), calls=%async_computation.3 | async-start | bytes 655360 | tf_op jit(solution)/shard_map/all_to_all | solution.py:273
  24.0 1.5 convolution_bitcast_fusion.2
  26.3 7.7 %all-to-all-done.3 = f32[1,320,168]{2,0,1:T(1,128)S(1)} async-done(((f32[1,320,168]{2,0,1:T(1,128)}), f32[1,320,168]{2,0,1:T(1,128)S(1)}, u32[]{:S(2)}, u32[]{:S(2)}) %all-to-all-start.3) | async-done | bytes 215072 | tf_op jit(solution)/shard_map/all_to_all | solution.py:273
  34.1 3.6 %all-to-all-start.1 = ((f32[1,320,168]{2,0,1:T(1,128)}), f32[1,320,168]{2,0,1:T(1,128)S(1)}, u32[]{:S(2)}, u32[]{:S(2)}) async-start(f32[1,320,168]{2,0,1:T(1,128)} %copy.126), calls=%async_computation.1 | async-start | bytes 655360 | tf_op jit(solution)/shard_map/all_to_all | solution.py:273
  38.8 6.2 %forward_rows.3 = f32[20,4,640]{2,1,0:T(4,128)S(1)} custom-call(f32[3,20]{1,0:T(4,128)S(1)} %get-tuple-element.35.facts, f32[20,48,64]{2,1,0:T(8,128)S(1)} %reshape.370.x_ref, f32[1,640]{1,0:T(1,128)S(1)} %convert_element_type.60.wave_ref), custom_call_target="tpu_custom_call" | custom-call | flops 4000000000 | bytes 2000000 | tf_op jit(solution)/shard_map/forward_rows/pallas_call | solution.py:279
  45.1 1.5 reshape.371
  46.6 1.7 copy.134
  48.3 2.9 %reshape.386 = f32[32,1,1600]{2,1,0:T(1,128)} reshape(f32[32,20,2,1,2,20]{5,4,2,1,0,3:T(2,128)S(1)} %copy.134) | data formatting | bytes 409600 | tf_op jit(solution)/shard_map/reshape | solution.py:221
  51.2 16.4 %all-to-all-start.4 = ((f32[32,1,1600]{2,1,0:T(1,128)}), f32[32,1,1600]{2,1,0:T(1,128)S(1)}, u32[]{:S(2)}, u32[]{:S(2)}) async-start(f32[32,1,1600]{2,1,0:T(1,128)} %reshape.386), calls=%async_computation.4 | async-start | bytes 425984 | tf_op jit(solution)/shard_map/all_to_all | solution.py:221
  68.6 6.2 %forward_rows.2 = f32[20,4,640]{2,1,0:T(4,128)S(1)} custom-call(f32[3,20]{1,0:T(4,128)S(1)} %get-tuple-element.34.facts, f32[20,48,64]{2,1,0:T(8,128)S(1)} %reshape.367.x_ref, f32[1,640]{1,0:T(1,128)S(1)} %convert_element_type.60.wave_ref), custom_call_target="tpu_custom_call" | custom-call | flops 4000000000 | bytes 2000000 | tf_op jit(solution)/shard_map/forward_rows/pallas_call | solution.py:279
  74.8 1.5 reshape.368
  76.3 1.7 copy.129
  78.0 2.9 %reshape.385 = f32[32,1,1600]{2,1,0:T(1,128)} reshape(f32[32,20,2,1,2,20]{5,4,2,1,0,3:T(2,128)S(1)} %copy.129) | data formatting | bytes 409600 | tf_op jit(solution)/shard_map/reshape | solution.py:221
  80.9 5.6 %all-to-all-start.2 = ((f32[32,1,1600]{2,1,0:T(1,128)}), f32[32,1,1600]{2,1,0:T(1,128)S(1)}, u32[]{:S(2)}, u32[]{:S(2)}) async-start(f32[32,1,1600]{2,1,0:T(1,128)} %reshape.385), calls=%async_computation.2 | async-start | bytes 425984 | tf_op jit(solution)/shard_map/all_to_all | solution.py:221
  87.5 2.1 stack_reshape_reshape.7
  89.7 6.2 %all-to-all-done.2 = f32[32,1,1600]{2,1,0:T(1,128)S(1)} async-done(((f32[32,1,1600]{2,1,0:T(1,128)}), f32[32,1,1600]{2,1,0:T(1,128)S(1)}, u32[]{:S(2)}, u32[]{:S(2)}) %all-to-all-start.2) | async-done | bytes 204832 | tf_op jit(solution)/shard_map/all_to_all | solution.py:221
  96.4 2.1 stack_reshape_reshape.6
  98.5 1.4 maximum_bitcast_fusion
  99.9 3.5 %copy.136 = f32[10,2,2,4,1,2,8,2,20]{8,7,6,5,3,2,1,0,4:T(2,128)} copy(f32[10,2,2,4,1,2,8,2,20]{8,5,2,1,0,3,6,7,4:T(2,128)S(1)} %maximum_bitcast_fusion) | data formatting | bytes 819200 | tf_op jit(solution)/shard_map/transpose | solution.py:292
  103.4 4.6 %reshape.373.four_ref = f32[10,32,320]{2,1,0:T(8,128)S(1)} reshape(f32[10,2,2,4,1,2,8,2,20]{8,7,6,5,3,2,1,0,4:T(2,128)} %copy.136) | data formatting | bytes 819200 | tf_op jit(solution)/shard_map/reshape | solution.py:293
  108.0 13.5 %legendre_both.1 = (f32[8,7040]{1,0:T(8,128)S(1)}, f32[10,32,320]{2,1,0:T(8,128)S(1)}) custom-call(s32[2]{0:T(128)S(1)} %pad_add_fusion.3.place, s32[40]{0:T(128)S(1)} %dynamic_slice.6.low, f32[10,32,320]{2,1,0:T(8,128)S(1)} %reshape.373.four_ref, f32[320,25640]{1,0:T(8,128)} %leg_ref.1, f32[8,8]{1,0:T(8,128)S(1)} %mul.64.modes_ref, ...), custom_call_target="tpu_custom_call" | custom-call | tf_op jit(solution)/shard_map/legendre_both/pallas_call | solution.py:306
  122.3 3.6 %all-to-all-start.5 = ((f32[4,2,7040]{2,1,0:T(2,128)}), f32[4,2,7040]{2,1,0:T(2,128)S(1)}, u32[]{:S(2)}, u32[]{:S(2)}) async-start(f32[4,2,7040]{2,1,0:T(2,128)} %reshape.374), calls=%async_computation.5 | async-start | bytes 450560 | tf_op jit(solution)/shard_map/all_to_all | solution.py:338
  125.9 4.1 %reshape.376 = f32[10,2,2,4,1,2,8,2,20]{8,7,6,5,3,2,1,0,4:T(2,128)S(1)} reshape(f32[10,32,320]{2,1,0:T(8,128)S(1)} %get-tuple-element.5) | data formatting | bytes 819200 | tf_op jit(solution)/shard_map/reshape | solution.py:333
  130.0 1.3 copy.164
  132.3 2.9 %reshape_squeeze.9 = f32[32,1,1600]{2,1,0:T(1,128)} reshape(f32[1,8,4,10,2,2,1,2,20]{8,7,5,4,3,2,1,6,0:T(2,128)S(1)} %get-tuple-element.21) | data formatting | bytes 409600 | tf_op jit(solution)/shard_map/reshape;squeeze | solution.py:221
  135.1 3.6 %all-to-all-start.8 = ((f32[32,1,1600]{2,1,0:T(1,128)}), f32[32,1,1600]{2,1,0:T(1,128)S(1)}, u32[]{:S(2)}, u32[]{:S(2)}) async-start(f32[32,1,1600]{2,1,0:T(1,128)} %reshape_squeeze.9), calls=%async_computation.8 | async-start | bytes 425984 | tf_op jit(solution)/shard_map/all_to_all | solution.py:221
  138.8 2.9 %reshape_squeeze.8 = f32[32,1,1600]{2,1,0:T(1,128)} reshape(f32[1,8,4,10,2,2,1,2,20]{8,7,5,4,3,2,1,6,0:T(2,128)S(1)} %get-tuple-element.20) | data formatting | bytes 409600 | tf_op jit(solution)/shard_map/reshape;squeeze | solution.py:221
  141.7 6.5 %all-to-all-done.8 = f32[32,1,1600]{2,1,0:T(1,128)S(1)} async-done(((f32[32,1,1600]{2,1,0:T(1,128)}), f32[32,1,1600]{2,1,0:T(1,128)S(1)}, u32[]{:S(2)}, u32[]{:S(2)}) %all-to-all-start.8) | async-done | bytes 204832 | tf_op jit(solution)/shard_map/all_to_all | solution.py:221
  148.2 3.0 %all-to-all-start.6 = ((f32[32,1,1600]{2,1,0:T(1,128)}), f32[32,1,1600]{2,1,0:T(1,128)S(1)}, u32[]{:S(2)}, u32[]{:S(2)}) async-start(f32[32,1,1600]{2,1,0:T(1,128)} %reshape_squeeze.8), calls=%async_computation.6 | async-start | bytes 425984 | tf_op jit(solution)/shard_map/all_to_all | solution.py:221
  151.7 2.1 reshape.380
  154.3 7.5 %inverse_rows.3 = f32[20,48,64]{2,1,0:T(8,128)S(1)} custom-call(f32[3,20]{1,0:T(4,128)S(1)} %get-tuple-element.35.facts, f32[20,4,640]{2,1,0:T(4,128)S(1)} %copy.157.f_ref, f32[1,640]{1,0:T(1,128)S(1)} %convert_element_type.60.wave_ref), custom_call_target="tpu_custom_call" | custom-call | flops 4000000000 | bytes 2000000 | tf_op jit(solution)/shard_map/inverse_rows/pallas_call | solution.py:351
  163.6 6.4 %reduce.4 = f32[1344,40]{1,0:T(8,128)S(1)} reduce(f32[1344,1,40]{2,1,0:T(1,128)S(1)} %bitcast.101, f32[]{:T(128)} %broadcast.185), dimensions={1}, to_apply=%bitcast.84.reduce_sub_computation | reduce | bytes 430084
  171.2 6.2 %all-to-all-start.9 = ((f32[8,1,6720]{2,1,0:T(1,128)}), f32[8,1,6720]{2,1,0:T(1,128)}, u32[]{:S(2)}, u32[]{:S(2)}) async-start(f32[8,1,6720]{2,1,0:T(1,128)} %reshape.400), calls=%async_computation.9 | async-start | bytes 434176 | tf_op jit(solution)/shard_map/all_to_all | solution.py:362
  179.8 1.4 reduce.2
  181.3 3.2 %reshape.377 = f32[32,20,2,1,2,20]{5,4,2,1,0,3:T(2,128)} reshape(f32[32,1600]{1,0:T(8,128)S(1)} %reduce.2) | data formatting | bytes 409600 | tf_op jit(solution)/shard_map/reshape | solution.py:222
  184.5 1.7 copy.155.f_ref
  186.2 7.5 %inverse_rows.2 = f32[20,48,64]{2,1,0:T(8,128)S(1)} custom-call(f32[3,20]{1,0:T(4,128)S(1)} %get-tuple-element.34.facts, f32[20,4,640]{2,1,0:T(4,128)S(1)} %copy.155.f_ref, f32[1,640]{1,0:T(1,128)S(1)} %convert_element_type.60.wave_ref), custom_call_target="tpu_custom_call" | custom-call | flops 4000000000 | bytes 2000000 | tf_op jit(solution)/shard_map/inverse_rows/pallas_call | solution.py:351
  194.9 6.4 %reduce.6 = f32[1344,40]{1,0:T(8,128)S(1)} reduce(f32[1344,1,40]{2,1,0:T(1,128)S(1)} %bitcast.102, f32[]{:T(128)} %broadcast.185), dimensions={1}, to_apply=%bitcast.86.reduce_sub_computation | reduce | bytes 430084
  202.6 6.2 %all-to-all-start.7 = ((f32[8,1,6720]{2,1,0:T(1,128)}), f32[8,1,6720]{2,1,0:T(1,128)S(1)}, u32[]{:S(2)}, u32[]{:S(2)}) async-start(f32[8,1,6720]{2,1,0:T(1,128)} %reshape.402), calls=%async_computation.7 | async-start | bytes 434176 | tf_op jit(solution)/shard_map/all_to_all | solution.py:362
  209.5 2.1 reduce.5
  213.4 3.4 %all-to-all-done.7 = f32[8,1,6720]{2,1,0:T(1,128)S(1)} async-done(((f32[8,1,6720]{2,1,0:T(1,128)}), f32[8,1,6720]{2,1,0:T(1,128)S(1)}, u32[]{:S(2)}, u32[]{:S(2)}) %all-to-all-start.7) | async-done | bytes 215072 | tf_op jit(solution)/shard_map/all_to_all | solution.py:362
  219.7 1.7 convolution_bitcast_fusion
  222.6 3.5 %all-to-all-start.10 = ((f32[1,640,168]{2,0,1:T(1,128)}), f32[1,640,168]{2,0,1:T(1,128)S(1)}, u32[]{:S(2)}, u32[]{:S(2)}) async-start(f32[1,640,168]{2,0,1:T(1,128)} %copy.152), calls=%async_computation.10 | async-start | bytes 1310720 | tf_op jit(solution)/shard_map/all_to_all | solution.py:365
  226.8 9.5 %all-to-all-done.10 = f32[1,640,168]{2,0,1:T(1,128)S(1)} async-done(((f32[1,640,168]{2,0,1:T(1,128)}), f32[1,640,168]{2,0,1:T(1,128)S(1)}, u32[]{:S(2)}, u32[]{:S(2)}) %all-to-all-start.10) | async-done | bytes 430112 | tf_op jit(solution)/shard_map/all_to_all | solution.py:365
  (92 shorter events, 30.1 us)
Async XLA Ops:
  0.6 14.5 %all-to-all-start = ((f32[4,160,168]{2,1,0:T(8,128)}), f32[4,160,168]{2,1,0:T(8,128)S(1)}, u32[]{:S(2)}, u32[]{:S(2)}) async-start(f32[4,160,168]{2,1,0:T(8,128)} %param.9), calls=%async_computation | async-start | bytes 1310720 | tf_op jit(solution)/shard_map/all_to_all | solution.py:269
  9.8 1.2 copy-start.5
  17.5 16.6 %all-to-all-start.3 = ((f32[1,320,168]{2,0,1:T(1,128)}), f32[1,320,168]{2,0,1:T(1,128)S(1)}, u32[]{:S(2)}, u32[]{:S(2)}) async-start(f32[1,320,168]{2,0,1:T(1,128)} %copy.132), calls=%async_computation.3 | async-start | bytes 655360 | tf_op jit(solution)/shard_map/all_to_all | solution.py:273
  34.1 17.1 %all-to-all-start.1 = ((f32[1,320,168]{2,0,1:T(1,128)}), f32[1,320,168]{2,0,1:T(1,128)S(1)}, u32[]{:S(2)}, u32[]{:S(2)}) async-start(f32[1,320,168]{2,0,1:T(1,128)} %copy.126), calls=%async_computation.1 | async-start | bytes 655360 | tf_op jit(solution)/shard_map/all_to_all | solution.py:273
  51.2 29.7 %all-to-all-start.4 = ((f32[32,1,1600]{2,1,0:T(1,128)}), f32[32,1,1600]{2,1,0:T(1,128)S(1)}, u32[]{:S(2)}, u32[]{:S(2)}) async-start(f32[32,1,1600]{2,1,0:T(1,128)} %reshape.386), calls=%async_computation.4 | async-start | bytes 425984 | tf_op jit(solution)/shard_map/all_to_all | solution.py:221
  76.3 10.3 %copy-start.6 = (f32[4,4]{1,0:T(4,128)S(1)}, f32[4,4]{1,0:T(4,128)}, u32[]{:S(2)}) copy-start(f32[4,4]{1,0:T(4,128)} %param.16) | copy-start | bytes 196
  76.3 10.3 %copy-start.7 = (f32[4,4]{1,0:T(4,128)S(1)}, f32[4,4]{1,0:T(4,128)}, u32[]{:S(2)}) copy-start(f32[4,4]{1,0:T(4,128)} %param.15) | copy-start | bytes 196
  78.0 8.8 %copy-start.8 = (f32[4]{0:T(128)S(1)}, f32[4]{0:T(128)}, u32[]{:S(2)}) copy-start(f32[4]{0:T(128)} %param.17) | copy-start | bytes 52
  80.9 15.0 %all-to-all-start.2 = ((f32[32,1,1600]{2,1,0:T(1,128)}), f32[32,1,1600]{2,1,0:T(1,128)S(1)}, u32[]{:S(2)}, u32[]{:S(2)}) async-start(f32[32,1,1600]{2,1,0:T(1,128)} %reshape.385), calls=%async_computation.2 | async-start | bytes 425984 | tf_op jit(solution)/shard_map/all_to_all | solution.py:221
  122.3 12.8 %all-to-all-start.5 = ((f32[4,2,7040]{2,1,0:T(2,128)}), f32[4,2,7040]{2,1,0:T(2,128)S(1)}, u32[]{:S(2)}, u32[]{:S(2)}) async-start(f32[4,2,7040]{2,1,0:T(2,128)} %reshape.374), calls=%async_computation.5 | async-start | bytes 450560 | tf_op jit(solution)/shard_map/all_to_all | solution.py:338
  135.1 13.0 %all-to-all-start.8 = ((f32[32,1,1600]{2,1,0:T(1,128)}), f32[32,1,1600]{2,1,0:T(1,128)S(1)}, u32[]{:S(2)}, u32[]{:S(2)}) async-start(f32[32,1,1600]{2,1,0:T(1,128)} %reshape_squeeze.9), calls=%async_computation.8 | async-start | bytes 425984 | tf_op jit(solution)/shard_map/all_to_all | solution.py:221
  148.2 23.1 %all-to-all-start.6 = ((f32[32,1,1600]{2,1,0:T(1,128)}), f32[32,1,1600]{2,1,0:T(1,128)S(1)}, u32[]{:S(2)}, u32[]{:S(2)}) async-start(f32[32,1,1600]{2,1,0:T(1,128)} %reshape_squeeze.8), calls=%async_computation.6 | async-start | bytes 425984 | tf_op jit(solution)/shard_map/all_to_all | solution.py:221
  162.1 15.3 %copy-start = (f32[320,2,640]{2,0,1:T(8,128)S(1)}, f32[320,2,640]{2,0,1:T(8,128)}, u32[]{:S(2)}) copy-start(f32[320,2,640]{2,0,1:T(8,128)} %get-tuple-element.22) | copy-start | bytes 4915204
  171.2 6.2 %copy-start.1 = (f32[32,1,1600]{2,1,0:T(1,128)}, f32[32,1,1600]{2,1,0:T(1,128)S(1)}, u32[]{:S(2)}) copy-start(f32[32,1,1600]{2,1,0:T(1,128)S(1)} %all-to-all-done.6) | copy-start | bytes 614404
  171.2 31.4 %all-to-all-start.9 = ((f32[8,1,6720]{2,1,0:T(1,128)}), f32[8,1,6720]{2,1,0:T(1,128)}, u32[]{:S(2)}, u32[]{:S(2)}) async-start(f32[8,1,6720]{2,1,0:T(1,128)} %reshape.400), calls=%async_computation.9 | async-start | bytes 434176 | tf_op jit(solution)/shard_map/all_to_all | solution.py:362
  202.6 14.2 %all-to-all-start.7 = ((f32[8,1,6720]{2,1,0:T(1,128)}), f32[8,1,6720]{2,1,0:T(1,128)S(1)}, u32[]{:S(2)}, u32[]{:S(2)}) async-start(f32[8,1,6720]{2,1,0:T(1,128)} %reshape.402), calls=%async_computation.7 | async-start | bytes 434176 | tf_op jit(solution)/shard_map/all_to_all | solution.py:362
  221.4 4.7 %copy-start.2 = (f32[2,7040]{1,0:T(2,128)S(1)}, f32[2,7040]{1,0:T(2,128)}, u32[]{:S(2)}) copy-start(f32[2,7040]{1,0:T(2,128)} %get-tuple-element.27) | copy-start | bytes 168964
  221.4 4.7 %copy-start.3 = (f32[2,7040]{1,0:T(2,128)S(1)}, f32[2,7040]{1,0:T(2,128)}, u32[]{:S(2)}) copy-start(f32[2,7040]{1,0:T(2,128)} %get-tuple-element.28) | copy-start | bytes 168964
  221.4 4.7 %copy-start.4 = (f32[2,7040]{1,0:T(2,128)S(1)}, f32[2,7040]{1,0:T(2,128)}, u32[]{:S(2)}) copy-start(f32[2,7040]{1,0:T(2,128)} %get-tuple-element.29) | copy-start | bytes 168964
  222.6 13.7 %all-to-all-start.10 = ((f32[1,640,168]{2,0,1:T(1,128)}), f32[1,640,168]{2,0,1:T(1,128)S(1)}, u32[]{:S(2)}, u32[]{:S(2)}) async-start(f32[1,640,168]{2,0,1:T(1,128)} %copy.152), calls=%async_computation.10 | async-start | bytes 1310720 | tf_op jit(solution)/shard_map/all_to_all | solution.py:365

commit v3 on v1

--- a/solution.py
+++ b/solution.py
@@ -12,7 +12,7 @@
 HIGHEST = lax.Precision.HIGHEST
 BOTH = ("wave", "lev")
 INNER = 64
-WIDTH = 512
+WIDTH = 640
 NN = (((1,), (0,)), ((), ()))
 NT = (((1,), (1,)), ((), ()))
 
@@ -79,14 +79,39 @@
     return (position.astype(jnp.float32) < length).astype(jnp.float32)
 
 
+def angle_sums(cos_base, sin_base, cos_step, sin_step):
+    cos_rows, sin_rows = [], []
+    for k in range(cos_step.shape[0]):
+        c, s = cos_step[k : k + 1], sin_step[k : k + 1]
+        cos_rows.append(cos_base * c - sin_base * s)
+        sin_rows.append(sin_base * c + cos_base * s)
+    return jnp.concatenate(cos_rows, axis=0), jnp.concatenate(sin_rows, axis=0)
+
+
 def tables(wave, length, inverse, outer):
-    inner_idx = row_iota(INNER).astype(jnp.float32)
-    outer_idx = (row_iota(outer) * INNER).astype(jnp.float32)
-    return turn(inner_idx * wave, length, inverse) + turn(outer_idx * wave, length, inverse)
+    row = row_iota(32)
+    scale = jnp.where(row < 16, jnp.where(row < 8, 1, 8), jnp.where(row < 24, 64, 512))
+    multiple = ((row & 7) * scale).astype(jnp.float32)
+    c, s = turn(multiple * wave, length, inverse)
+    top = 24 + outer // 8
+    return angle_sums(c[:8], s[:8], c[8:16], s[8:16]) + angle_sums(
+        c[16:24], s[16:24], c[24:top], s[24:top]
+    )
+
+
+def each_row(rows, one):
+    together = 2 if rows % 2 == 0 else 1
+
+    def some(step, carry):
+        for k in range(together):
+            one(step * together + k)
+        return carry
+
+    lax.fori_loop(0, rows // together, some, 0)
 
 
 def forward_kernel(vectors, outer, facts, x_ref, wave_ref, out_ref):
-    def one(r, carry):
+    def one(r):
         length, inverse, norm = facts[0, r], facts[1, r], facts[2, r]
         wave = wave_ref[...]
         cos_in, sin_in, cos_out, sin_out = tables(wave, length, inverse, outer)
@@ -101,13 +126,12 @@
             rows.append(jnp.sum(p * cos_out - q * sin_out, axis=0, keepdims=True) * keep)
             rows.append(jnp.sum(q * cos_out + p * sin_out, axis=0, keepdims=True) * -keep)
         out_ref[r] = jnp.concatenate(rows, axis=0)
-        return carry
-
-    lax.fori_loop(0, x_ref.shape[0], one, 0)
+
+    each_row(x_ref.shape[0], one)
 
 
 def inverse_kernel(vectors, outer, scale, facts, f_ref, wave_ref, out_ref):
-    def one(r, carry):
+    def one(r):
         length, inverse, norm = facts[0, r], facts[1, r], facts[2, r]
         wave = wave_ref[...]
         cos_in, sin_in, cos_out, sin_out = tables(wave, length, inverse, outer)
@@ -122,23 +146,23 @@
         values = dot_split(*both_halves(jnp.concatenate(real, axis=0)), *halves(cos_in), NT)
         values += dot_split(*both_halves(jnp.concatenate(imaginary, axis=0)), *halves(sin_in), NT)
         out_ref[r] = values * live_mask(length, vectors, outer)
-        return carry
-
-    lax.fori_loop(0, f_ref.shape[0], one, 0)
+
+    each_row(f_ref.shape[0], one)
 
 
 def legendre_kernel(
-    waves, used, span, place, low, four_ref, leg_ref, modes_ref, back_ref, rates_ref, spec_ref, out_ref
+    waves, used, span, place, low, sym_ref, anti_ref, leg_ref, modes_ref, back_ref, rates_ref, spec_ref, even_ref, odd_ref
 ):
     step = pl.program_id(0)
-    rows = four_ref.shape[1]
-    fields = rows // 4
+    rows = sym_ref.shape[1]
+    fields = rows // 2
     pair_total = low.shape[0]
     first_pair = place[1]
 
     @pl.when(step == 0)
     def _():
-        out_ref[...] = jnp.zeros_like(out_ref)
+        even_ref[...] = jnp.zeros_like(even_ref)
+        odd_ref[...] = jnp.zeros_like(odd_ref)
 
     base = (place[0] + step) * WIDTH
     pair = base // (waves + 1)
@@ -152,7 +176,7 @@
     inside = column - own_pair * (waves + 1)
     low_length = waves - low_wave
     upper = inside >= low_length
-    kind = jnp.where(upper, 2 + ((inside - low_length) & 1), inside & 1)
+    kind = jnp.where(upper, 1 + 2 * ((inside - low_length) & 1), 2 * (inside & 1))
     degree = jnp.where(upper, inside - 1, low_wave + inside).astype(jnp.float32)
     valid = (own_pair >= first_pair) & (own_pair < first_pair + span) & (column < used)
     kind = jnp.where(valid, jnp.where(second, kind + 4, kind), 8)
@@ -162,7 +186,9 @@
     there = jnp.clip(pair + 1 - first_pair, 0, span - 1)
     leg = jnp.where(column < used, leg_ref[...], 0.0)
     leg_high, leg_low = halves(leg)
-    four = jnp.concatenate([four_ref[here], four_ref[there]], axis=0)
+    four = jnp.concatenate(
+        [sym_ref[here], anti_ref[here], sym_ref[there], anti_ref[there]], axis=0
+    )
     product = dot_split(*both_halves(four), leg_high, leg_low, NN)
     raw = masks[0] * product[:fields]
     for s in range(1, 8):
@@ -179,8 +205,10 @@
     spec_ref[...] = spectral
     parts = jnp.concatenate([masks[s] * spectral for s in range(8)], axis=0)
     sums = dot_split(*both_halves(parts), leg_high, leg_low, NT)
-    out_ref[here] += sums[:rows]
-    out_ref[there] += sums[rows:]
+    even_ref[here] += sums[:rows]
+    odd_ref[here] += sums[rows : 2 * rows]
+    even_ref[there] += sums[2 * rows : 3 * rows]
+    odd_ref[there] += sums[3 * rows :]
 
 
 def smem():
@@ -202,20 +230,20 @@
 def body(
     n_wave, n_lev, grid, row_points, lat_of_slot, pair_low, legendre, lat_weight, vert_modes, vert_back, vert_rates
 ):
-    levels = grid.shape[0]
+    levels, slots_lev, chunk = grid.shape
     ld = levels // n_lev
     waves = lat_of_slot.shape[0]
     half = waves // 2
-    points = grid.shape[2] * n_wave
-    lats = half // n_wave
+    points = chunk * n_wave
     pair_count = legendre.shape[1] // (waves + 1)
     used = pair_count * (waves + 1)
     modes_pad = (used + 127) // 128 * 128
     span = -(-pair_count // n_lev)
     outer = -(-points // (INNER * 8)) * 8
-    vectors = 2 * ld
     fields = 2 * levels
     devices = n_wave * n_lev
+    some = -(-slots_lev // n_wave)
+    spare = n_wave * some - slots_lev
     wave_index = lax.axis_index("wave")
     lev_index = lax.axis_index("lev")
 
@@ -226,36 +254,43 @@
     )
     order = order.reshape(1, devices * span * 2).astype(jnp.float32)
     columns = order.shape[1]
-    my_points = lax.dynamic_slice_in_dim(row_points, wave_index * lats, lats).astype(jnp.float32)
+    blocks = jnp.pad(grid, ((0, 0), (0, spare), (0, 0))).reshape(levels, n_wave, some, chunk)
+    blocks = blocks.transpose(1, 0, 2, 3).reshape(n_wave, levels * some, chunk)
+    rows_in = lax.all_to_all(blocks, "wave", split_axis=0, concat_axis=0, tiled=True)
+
+    held = jnp.minimum(wave_index * some + jnp.arange(some), slots_lev - 1)
+    my_points = row_points[lat_of_slot[lev_index * slots_lev + held]].astype(jnp.float32)
     facts = jnp.stack([my_points, 1.0 / my_points, lax.rsqrt(my_points)])
 
+    lat_held = jnp.pad(
+        lat_of_slot.reshape(n_lev, slots_lev), ((0, 0), (0, spare)), constant_values=-1
+    ).reshape(1, -1)
+    slots = lat_held.shape[1]
     lat_idx = jnp.arange(half, dtype=jnp.int32)[:, None]
-    north = (lat_of_slot[None, :] == lat_idx).astype(jnp.float32)
-    south = (lat_of_slot[None, :] == waves - 1 - lat_idx).astype(jnp.float32)
-    unfold = jnp.stack([north + south, north - south], axis=1)
-    fold = (unfold * lat_weight[:, None, None]).reshape(waves, waves)
-    unfold = unfold.reshape(waves, waves)
-
-    whole = lax.all_to_all(grid, "lev", split_axis=0, concat_axis=1, tiled=True)
-    folded = jnp.einsum("xs,lsj->lxj", fold, whole, precision=HIGHEST)
-    rows_in = lax.all_to_all(folded, "wave", split_axis=1, concat_axis=2, tiled=True)
-    rows_in = rows_in.reshape(ld, lats, 2, points).transpose(1, 2, 0, 3)
-    rows_in = jnp.pad(rows_in, ((0, 0), (0, 0), (0, 0), (0, outer * INNER - points)))
-    rows_in = rows_in.reshape(lats, vectors * outer, INNER)
+    north = (lat_held == lat_idx).astype(jnp.float32)
+    south = (lat_held == waves - 1 - lat_idx).astype(jnp.float32)
+    both, apart = north + south, north - south
 
     params = pltpu.CompilerParams(vmem_limit_bytes=48 * 1024 * 1024)
+    rows_in = rows_in.reshape(n_wave, levels, some, chunk).transpose(2, 1, 0, 3)
+    rows_in = rows_in.reshape(some, levels, points)
+    rows_in = jnp.pad(rows_in, ((0, 0), (0, 0), (0, outer * INNER - points)))
+    rows_in = rows_in.reshape(some, levels * outer, INNER)
     fourier = pl.pallas_call(
-        functools.partial(forward_kernel, vectors, outer),
-        out_shape=jax.ShapeDtypeStruct((lats, 2 * vectors, columns), jnp.float32),
+        functools.partial(forward_kernel, levels, outer),
+        out_shape=jax.ShapeDtypeStruct((some, fields, columns), jnp.float32),
         in_specs=[smem(), vmem(), vmem()],
         out_specs=vmem(),
         compiler_params=params,
         name="forward_rows",
     )(facts, rows_in, order)
-
-    fourier = fourier.reshape(lats, 2, ld, 2, devices, 2 * span).transpose(4, 5, 1, 2, 3, 0)
-    arrived = exchange(fourier, BOTH).reshape(n_wave, n_lev, span, 2, 2, ld, 2, lats)
-    four = arrived.transpose(2, 3, 4, 1, 5, 6, 0, 7).reshape(span, 4 * fields, half)
+    fourier = fourier.reshape(some, fields, devices, 2 * span).transpose(2, 3, 1, 0)
+    arrived = exchange(fourier, BOTH).reshape(n_wave, n_lev, 2 * span * fields, some)
+    arrived = arrived.transpose(2, 1, 0, 3).reshape(2 * span * fields, slots)
+    symmetric = jnp.einsum("cs,rs->cr", arrived, both, precision=HIGHEST) * lat_weight
+    antisymmetric = jnp.einsum("cs,rs->cr", arrived, apart, precision=HIGHEST) * lat_weight
+    symmetric = symmetric.reshape(span, 2 * fields, half)
+    antisymmetric = antisymmetric.reshape(span, 2 * fields, half)
 
     starts = [min(l * span * (waves + 1), used - 1) // WIDTH for l in range(n_lev)]
     stops = [-(-min((l + 1) * span * (waves + 1), used) // WIDTH) for l in range(n_lev)]
@@ -268,17 +303,19 @@
     grow = lambda m: (m[:, None, :, None] * pair_eye[None, :, None, :]).reshape(fields, fields)
     rates = jnp.repeat(vert_rates, 2)[:, None]
     fixed = lambda *shape: pl.BlockSpec(shape, lambda t, *_: (0,) * len(shape))
-    spec, back = pl.pallas_call(
+    spec, even, odd = pl.pallas_call(
         functools.partial(legendre_kernel, waves, used, span),
         out_shape=(
             jax.ShapeDtypeStruct((fields, steps * WIDTH), jnp.float32),
-            jax.ShapeDtypeStruct((span, 4 * fields, half), jnp.float32),
+            jax.ShapeDtypeStruct((span, 2 * fields, half), jnp.float32),
+            jax.ShapeDtypeStruct((span, 2 * fields, half), jnp.float32),
         ),
         grid_spec=pltpu.PrefetchScalarGridSpec(
             num_scalar_prefetch=2,
             grid=(steps,),
             in_specs=[
-                fixed(span, 4 * fields, half),
+                fixed(span, 2 * fields, half),
+                fixed(span, 2 * fields, half),
                 pl.BlockSpec(
                     (half, WIDTH), lambda t, p, _: (0, jnp.minimum(p[0] + t, final_block))
                 ),
@@ -288,12 +325,18 @@
             ],
             out_specs=[
                 pl.BlockSpec((fields, WIDTH), lambda t, *_: (0, t)),
-                fixed(span, 4 * fields, half),
+                fixed(span, 2 * fields, half),
+                fixed(span, 2 * fields, half),
             ],
         ),
         compiler_params=params,
         name="legendre_both",
-    )(place, my_low, four, legendre, grow(vert_modes), grow(vert_back), rates)
+    )(place, my_low, symmetric, antisymmetric, legendre, grow(vert_modes), grow(vert_back), rates)
+
+    by_slot = jnp.einsum("cfr,rs->cfs", even, both, precision=HIGHEST)
+    by_slot += jnp.einsum("cfr,rs->cfs", odd, apart, precision=HIGHEST)
+    by_slot = by_slot.reshape(2 * span * fields, n_lev, n_wave, some).transpose(2, 1, 0, 3)
+    returned = exchange(by_slot.reshape(devices, 2 * span, fields, some), BOTH)
 
     pieces = lax.all_to_all(
         spec.reshape(n_lev, fields // n_lev, steps * WIDTH), "lev", split_axis=0, concat_axis=0, tiled=True
@@ -305,22 +348,21 @@
     )
     spectral = spectral[:, :modes_pad].reshape(ld, 2, modes_pad)
 
-    back = back.reshape(span, 2, 2, n_lev, ld, 2, n_wave, lats).transpose(6, 3, 0, 1, 2, 4, 5, 7)
-    returned = exchange(back.reshape(devices, 2 * span, 2, ld, 2, lats), BOTH)
-    returned = returned.transpose(5, 2, 3, 4, 0, 1).reshape(lats, 2 * vectors, columns)
+    returned = returned.transpose(3, 2, 0, 1).reshape(some, fields, columns)
     values = pl.pallas_call(
-        functools.partial(inverse_kernel, vectors, outer, 1.0 / math.sqrt(waves)),
-        out_shape=jax.ShapeDtypeStruct((lats, vectors * outer, INNER), jnp.float32),
+        functools.partial(inverse_kernel, levels, outer, 1.0 / math.sqrt(waves)),
+        out_shape=jax.ShapeDtypeStruct((some, levels * outer, INNER), jnp.float32),
         in_specs=[smem(), vmem(), vmem()],
         out_specs=vmem(),
         compiler_params=params,
         name="inverse_rows",
     )(facts, returned, order)
-    values = values.reshape(lats, 2, ld, outer * INNER)[..., :points]
-    values = values.transpose(2, 0, 1, 3).reshape(ld, 2 * lats, points)
-    values = lax.all_to_all(values, "wave", split_axis=2, concat_axis=1, tiled=True)
-    slots = jnp.einsum("xs,lxj->lsj", unfold, values, precision=HIGHEST)
-    grid_out = lax.all_to_all(slots, "lev", split_axis=1, concat_axis=0, tiled=True)
+    values = values.reshape(some, levels, outer * INNER)[..., :points]
+    values = values.reshape(some, levels, n_wave, chunk).transpose(2, 1, 0, 3)
+    values = values.reshape(n_wave, levels * some, chunk)
+    values = lax.all_to_all(values, "wave", split_axis=0, concat_axis=0, tiled=True)
+    values = values.reshape(n_wave, levels, some, chunk).transpose(1, 0, 2, 3)
+    grid_out = values.reshape(levels, n_wave * some, chunk)[:, :slots_lev]
     return spectral, grid_out
 
 

time: 214 us -> 170 us (0.79)
  Pallas kernels: 53.1 us -> 31.4 us
  waiting for transfers between devices: 77.7 us -> 62.4 us
  starting transfers between devices: 28 us -> 21.9 us
  other arithmetic: 3.52 us -> 0.92 us
    pallas_call x2, Pallas kernels: 37.8 us -> 17.9 us  [the longest x1 9.49 us: body(): pl.pallas_call(functools.partial(inverse_kernel, levels, outer, 1.0 / mat...]
    all_to_all x4 -> x2, waiting for transfers between devices: 48.1 us -> 32.3 us  [the longest x1 16.9 us: body(): lax.all_to_all(values, 'wave', split_axis=0, concat_axis=0, tiled=True)]
    all_to_all x4 -> x2, starting transfers between devices: 17.9 us -> 10.8 us  [the longest x1 7.25 us: body(): lax.all_to_all(blocks, 'wave', split_axis=0, concat_axis=0, tiled=True)]
    mul x2 -> x0, local copies, waits for them, and re-layouts: 4.88 us -> none  [body(): fold = (unfold * lat_weight[:, None, None]).reshape(waves, waves)]
    reshape x7 -> x12, local copies, waits for them, and re-layouts: 9.24 us -> 14 us  [the longest x1 4.56 us: body(): fourier.reshape(some, fields, devices, 2 * span).transpose(2, 3, 1, 0)]
    another operation x5 -> x1, local copies, waits for them, and re-layouts: 7.33 us -> 3.2 us  [body(): exchange(fourier, BOTH).reshape(n_wave, n_lev, 2 * span * fields, some)]
    transpose x3 -> x5, local copies, waits for them, and re-layouts: 5.07 us -> 8.89 us  [the longest x1 3.6 us: body(): fourier.reshape(some, fields, devices, 2 * span).transpose(2, 3, 1, 0)]
    dot_general x2 -> x4, matrix products: 5.17 us -> 6.95 us  [the longest x1 2.36 us: body(): jnp.einsum('cs,rs->cr', arrived, both, precision=HIGHEST) * lat_weight]
  transfers between devices with their start and end apart: 7 -> 5, of which waited for: 6 -> 4; matrix products, arithmetic and copies ran while one was open for 10% -> 9% of each run, Pallas kernels for 9% -> 0%
where the time goes in v3:
time: 170 us; the launch traced here: 169 us
  waiting for transfers between devices  62.4 us (37%)
  local copies, waits for them, and re-layouts  44.4 us (26%)
  Pallas kernels  31.4 us (18%)
  starting transfers between devices  21.9 us (13%)
  matrix products  6.95 us (4%)
    all_to_all x2, waiting for transfers between devices, exchange(): lax.all_to_all(blocks.reshape(dense), axes, split_axis=0, concat_axis=0,...  30 us
    all_to_all x1, waiting for transfers between devices, body(): lax.all_to_all(values, 'wave', split_axis=0, concat_axis=0, tiled=True)  16.9 us
    all_to_all x1, waiting for transfers between devices, body(): lax.all_to_all(blocks, 'wave', split_axis=0, concat_axis=0, tiled=True)  15.5 us
    pallas_call x1, Pallas kernels, body(): pl.pallas_call(functools.partial(legendre_kernel, waves, used, span), out...  13.5 us
    pallas_call x1, Pallas kernels, body(): pl.pallas_call(functools.partial(inverse_kernel, levels, outer, 1.0 / mat...  9.49 us
    pallas_call x1, Pallas kernels, body(): pl.pallas_call(functools.partial(forward_kernel, levels, outer), out_shap...  8.46 us
    all_to_all x2, starting transfers between devices, exchange(): lax.all_to_all(blocks.reshape(dense), axes, split_axis=0, concat_axis=0,...  7.54 us
    all_to_all x1, starting transfers between devices, body(): lax.all_to_all(blocks, 'wave', split_axis=0, concat_axis=0, tiled=True)  7.25 us
  transfers between devices with their start and end apart: 5, of which 4 were waited for; matrix products, arithmetic and copies ran while one was open for 9% of the time, Pallas kernels for 0%

profile of v3, /device:TPU:0, one launch (start us, length us, event | category | flops | bytes accessed | tf_op | source)
XLA Modules:
  0.0 169.0 jit_solution(7026488346776849194)
XLA Ops:
  0.7 1.5 copy.36
  2.2 0.4 copy.37
  2.6 1.0 copy.38
  3.6 7.3 %all-to-all-start = ((f32[8,80,168]{2,1,0:T(8,128)}), f32[8,80,168]{2,1,0:T(8,128)S(1)}, u32[]{:S(2)}, u32[]{:S(2)}) async-start(f32[8,80,168]{2,1,0:T(8,128)} %copy.38), calls=%async_computation | async-start | bytes 1310720 | tf_op jit(solution)/shard_map/all_to_all | solution.py:259
  10.9 0.7 gather_fusion
  11.7 0.1 copy.41
  11.8 0.1 convert_element_type.54.wave_ref
  12.0 0.7 gather_fusion.1
  12.7 15.5 %all-to-all-done = f32[8,80,168]{2,1,0:T(8,128)S(1)} async-done(((f32[8,80,168]{2,1,0:T(8,128)}), f32[8,80,168]{2,1,0:T(8,128)S(1)}, u32[]{:S(2)}, u32[]{:S(2)}) %all-to-all-start) | async-done | bytes 430112 | tf_op jit(solution)/shard_map/all_to_all | solution.py:259
  28.2 0.4 copy.39
  28.6 0.3 reshape.212
  28.9 0.1 copy.52
  29.0 0.1 pad.20
  29.1 0.4 reshape.178.x_ref
  29.5 8.5 %forward_rows.1 = f32[20,8,640]{2,1,0:T(8,128)S(1)} custom-call(f32[3,20]{1,0:T(4,128)S(1)} %pad_maximum_fusion.facts, f32[20,96,64]{2,1,0:T(8,128)S(1)} %reshape.178.x_ref, f32[1,640]{1,0:T(1,128)S(1)} %convert_element_type.54.wave_ref), custom_call_target="tpu_custom_call" | custom-call | tf_op jit(solution)/shard_map/forward_rows/pallas_call | solution.py:279
  37.9 4.6 %reshape.179 = f32[20,8,32,20]{3,2,1,0:T(8,128)} reshape(f32[20,8,640]{2,1,0:T(8,128)S(1)} %forward_rows.1) | data formatting | bytes 819200 | tf_op jit(solution)/shard_map/reshape | solution.py:287
  42.5 3.6 %copy.42 = f32[32,20,8,20]{3,2,1,0:T(8,128)S(1)} copy(f32[32,20,8,20]{1,0,2,3:T(8,128)} %bitcast.68) | data formatting | bytes 819200 | tf_op jit(solution)/shard_map/transpose | solution.py:287
  46.1 3.1 %reshape.180 = f32[32,25,128]{2,1,0:T(8,128)} reshape(f32[32,20,8,20]{3,2,1,0:T(8,128)S(1)} %copy.42) | data formatting | bytes 819200 | tf_op jit(solution)/shard_map/reshape | solution.py:226
  49.2 3.9 %all-to-all-start.1 = ((f32[32,25,128]{2,1,0:T(8,128)}), f32[32,25,128]{2,1,0:T(8,128)S(1)}, u32[]{:S(2)}, u32[]{:S(2)}) async-start(f32[32,25,128]{2,1,0:T(8,128)} %reshape.180), calls=%async_computation.1 | async-start | bytes 1048576 | tf_op jit(solution)/shard_map/all_to_all | solution.py:226
  53.4 0.1 mul.78.back_ref
  53.5 0.1 mul.75.modes_ref
  53.7 14.8 %all-to-all-done.1 = f32[32,25,128]{2,1,0:T(8,128)S(1)} async-done(((f32[32,25,128]{2,1,0:T(8,128)}), f32[32,25,128]{2,1,0:T(8,128)S(1)}, u32[]{:S(2)}, u32[]{:S(2)}) %all-to-all-start.1) | async-done | bytes 409632 | tf_op jit(solution)/shard_map/all_to_all | solution.py:226
  68.5 3.2 %reshape_reshape.6 = f32[8,4,160,20]{3,2,1,0:T(8,128)S(1)} reshape(f32[32,25,128]{2,1,0:T(8,128)S(1)} %all-to-all-done.1) | data formatting | bytes 819200 | tf_op jit(solution)/shard_map/reshape;reshape | solution.py:288
  71.7 1.5 copy.43
  73.2 2.4 %convolution_multiply_fusion = f32[160,320]{1,0:T(8,128)S(1)} fusion(f32[160,640]{0,1:T(8,128)S(1)} %reshape.181, s32[640]{0:T(1024)S(1)} %copy-done.2, s32[320]{0:T(512)S(1)} %iota_subtract_fusion, f32[320]{0:T(512)S(1)} %copy-done.3), kind=kOutput, calls=%fused_computation.3 | convolution fusion | flops 394291200 | bytes 619520 | tf_op jit(solution)/shard_map/cs,rs->cr/dot_general | solution.py:291
  75.6 2.4 %convolution_multiply_fusion.1 = f32[160,320]{1,0:T(8,128)S(1)} fusion(f32[160,640]{0,1:T(8,128)S(1)} %reshape.181, s32[640]{0:T(1024)S(1)} %copy-done.2, s32[320]{0:T(512)S(1)} %iota_subtract_fusion, f32[320]{0:T(512)S(1)} %copy-done.3), kind=kOutput, calls=%fused_computation.4 | convolution fusion | flops 394291200 | bytes 619520 | tf_op jit(solution)/shard_map/cs,rs->cr/dot_general | solution.py:290
  78.0 13.5 %legendre_both.1 = (f32[8,7040]{1,0:T(8,128)S(1)}, f32[10,16,320]{2,1,0:T(8,128)S(1)}, f32[10,16,320]{2,1,0:T(8,128)S(1)}) custom-call(s32[2]{0:T(128)S(1)} %pad_add_fusion.3.place, s32[40]{0:T(128)S(1)} %dynamic_slice.3.low, f32[10,16,320]{2,1,0:T(8,128)S(1)} %bitcast.67, f32[10,16,320]{2,1,0:T(8,128)S(1)} %bitcast.66, f32[320,25640]{1,0:T(8,128)} %leg_ref.1, ...), custom_call_target="tpu_custom_call" | custom-call | tf_op jit(solution)/shard_map/legendre_both/pallas_call | solution.py:306
  91.5 0.8 reshape.184
  92.3 3.6 %all-to-all-start.2 = ((f32[4,2,7040]{2,1,0:T(2,128)}), f32[4,2,7040]{2,1,0:T(2,128)S(1)}, u32[]{:S(2)}, u32[]{:S(2)}) async-start(f32[4,2,7040]{2,1,0:T(2,128)} %reshape.184), calls=%async_computation.2 | async-start | bytes 450560 | tf_op jit(solution)/shard_map/all_to_all | solution.py:341
  95.9 1.1 fusion.3
  97.0 1.1 convolution_add_fusion
  98.2 3.0 %reshape.186 = f32[160,4,8,20]{3,2,1,0:T(8,128)S(1)} reshape(f32[10,16,640]{2,1,0:T(8,128)S(1)} %convolution_add_fusion) | data formatting | bytes 819200 | tf_op jit(solution)/shard_map/reshape | solution.py:338
  101.2 3.0 %copy.45 = f32[8,4,160,20]{3,2,1,0:T(8,128)} copy(f32[8,4,160,20]{3,0,1,2:T(8,128)S(1)} %bitcast.70) | data formatting | bytes 819200 | tf_op jit(solution)/shard_map/transpose | solution.py:338
  104.2 4.2 %reshape_reshape.7 = f32[32,25,128]{2,1,0:T(8,128)} reshape(f32[8,4,160,20]{3,2,1,0:T(8,128)} %copy.45) | data formatting | bytes 819200 | tf_op jit(solution)/shard_map/reshape;reshape | solution.py:226
  108.5 3.6 %all-to-all-start.3 = ((f32[32,25,128]{2,1,0:T(8,128)}), f32[32,25,128]{2,1,0:T(8,128)S(1)}, u32[]{:S(2)}, u32[]{:S(2)}) async-start(f32[32,25,128]{2,1,0:T(8,128)} %reshape_reshape.7), calls=%async_computation.3 | async-start | bytes 1048576 | tf_op jit(solution)/shard_map/all_to_all | solution.py:226
  112.1 15.3 %all-to-all-done.3 = f32[32,25,128]{2,1,0:T(8,128)S(1)} async-done(((f32[32,25,128]{2,1,0:T(8,128)}), f32[32,25,128]{2,1,0:T(8,128)S(1)}, u32[]{:S(2)}, u32[]{:S(2)}) %all-to-all-start.3) | async-done | bytes 409632 | tf_op jit(solution)/shard_map/all_to_all | solution.py:226
  127.4 4.7 %reshape.187 = f32[32,20,8,20]{3,2,1,0:T(8,128)} reshape(f32[32,25,128]{2,1,0:T(8,128)S(1)} %all-to-all-done.3) | data formatting | bytes 819200 | tf_op jit(solution)/shard_map/reshape | solution.py:227
  132.1 2.5 %copy.53.f_ref = f32[20,8,640]{2,1,0:T(8,128)S(1)} copy(f32[20,8,640]{0,1,2:T(8,128)} %bitcast.71) | data formatting | bytes 819200 | tf_op jit(solution)/shard_map/reshape | solution.py:351
  134.6 9.5 %inverse_rows.1 = f32[20,96,64]{2,1,0:T(8,128)S(1)} custom-call(f32[3,20]{1,0:T(4,128)S(1)} %pad_maximum_fusion.facts, f32[20,8,640]{2,1,0:T(8,128)S(1)} %copy.53.f_ref, f32[1,640]{1,0:T(1,128)S(1)} %convert_element_type.54.wave_ref), custom_call_target="tpu_custom_call" | custom-call | tf_op jit(solution)/shard_map/inverse_rows/pallas_call | solution.py:352
  144.1 0.3 reshape.189
  144.5 0.5 reshape.190
  145.1 1.0 copy.48
  146.1 3.5 %all-to-all-start.4 = ((f32[8,80,168]{2,1,0:T(8,128)}), f32[8,80,168]{2,1,0:T(8,128)S(1)}, u32[]{:S(2)}, u32[]{:S(2)}) async-start(f32[8,80,168]{2,1,0:T(8,128)} %copy.48), calls=%async_computation.4 | async-start | bytes 1310720 | tf_op jit(solution)/shard_map/all_to_all | solution.py:363
  149.7 0.7 fusion.13
  150.4 16.9 %all-to-all-done.4 = f32[8,80,168]{2,1,0:T(8,128)S(1)} async-done(((f32[8,80,168]{2,1,0:T(8,128)}), f32[8,80,168]{2,1,0:T(8,128)S(1)}, u32[]{:S(2)}, u32[]{:S(2)}) %all-to-all-start.4) | async-done | bytes 430112 | tf_op jit(solution)/shard_map/all_to_all | solution.py:363
  167.2 0.4 copy.49
  167.6 0.4 copy.50
  168.1 1.0 copy.51
  (38 shorter events, 0.8 us)
Async XLA Ops:
  0.6 11.4 %copy-start = (s32[640]{0:T(1024)S(1)}, s32[640]{0:T(1024)}, u32[]{:S(2)}) copy-start(s32[640]{0:T(1024)} %param.10) | copy-start | bytes 7684
  0.6 10.3 %copy-start.2 = (s32[640]{0:T(1024)S(1)}, s32[640]{0:T(1024)}, u32[]{:S(2)}) copy-start(s32[640]{0:T(1024)} %param.11) | copy-start | bytes 7684
  0.7 10.9 %copy-start.4 = (s32[320]{0:T(512)S(1)}, s32[320]{0:T(512)}, u32[]{:S(2)}) copy-start(s32[320]{0:T(512)} %param.12) | copy-start | bytes 3844
  3.6 24.5 %all-to-all-start = ((f32[8,80,168]{2,1,0:T(8,128)}), f32[8,80,168]{2,1,0:T(8,128)S(1)}, u32[]{:S(2)}, u32[]{:S(2)}) async-start(f32[8,80,168]{2,1,0:T(8,128)} %copy.38), calls=%async_computation | async-start | bytes 1310720 | tf_op jit(solution)/shard_map/all_to_all | solution.py:259
  46.1 7.1 %copy-start.7 = (f32[4]{0:T(128)S(1)}, f32[4]{0:T(128)}, u32[]{:S(2)}) copy-start(f32[4]{0:T(128)} %param.17) | copy-start | bytes 52
  46.1 7.2 %copy-start.5 = (f32[4,4]{1,0:T(4,128)S(1)}, f32[4,4]{1,0:T(4,128)}, u32[]{:S(2)}) copy-start(f32[4,4]{1,0:T(4,128)} %param.16) | copy-start | bytes 196
  46.1 7.2 %copy-start.6 = (f32[4,4]{1,0:T(4,128)S(1)}, f32[4,4]{1,0:T(4,128)}, u32[]{:S(2)}) copy-start(f32[4,4]{1,0:T(4,128)} %param.15) | copy-start | bytes 196
  49.2 19.3 %all-to-all-start.1 = ((f32[32,25,128]{2,1,0:T(8,128)}), f32[32,25,128]{2,1,0:T(8,128)S(1)}, u32[]{:S(2)}, u32[]{:S(2)}) async-start(f32[32,25,128]{2,1,0:T(8,128)} %reshape.180), calls=%async_computation.1 | async-start | bytes 1048576 | tf_op jit(solution)/shard_map/all_to_all | solution.py:226
  71.7 1.6 copy-start.3
  92.3 16.1 %all-to-all-start.2 = ((f32[4,2,7040]{2,1,0:T(2,128)}), f32[4,2,7040]{2,1,0:T(2,128)S(1)}, u32[]{:S(2)}, u32[]{:S(2)}) async-start(f32[4,2,7040]{2,1,0:T(2,128)} %reshape.184), calls=%async_computation.2 | async-start | bytes 450560 | tf_op jit(solution)/shard_map/all_to_all | solution.py:341
  108.5 18.9 %all-to-all-start.3 = ((f32[32,25,128]{2,1,0:T(8,128)}), f32[32,25,128]{2,1,0:T(8,128)S(1)}, u32[]{:S(2)}, u32[]{:S(2)}) async-start(f32[32,25,128]{2,1,0:T(8,128)} %reshape_reshape.7), calls=%async_computation.3 | async-start | bytes 1048576 | tf_op jit(solution)/shard_map/all_to_all | solution.py:226
  145.1 23.9 %copy-start.1 = (s32[640]{0:T(1024)S(1)}, s32[640]{0:T(1024)}, u32[]{:S(2)}) copy-start(s32[640]{0:T(1024)} %param.10) | copy-start | bytes 7684
  146.1 21.1 %all-to-all-start.4 = ((f32[8,80,168]{2,1,0:T(8,128)}), f32[8,80,168]{2,1,0:T(8,128)S(1)}, u32[]{:S(2)}, u32[]{:S(2)}) async-start(f32[8,80,168]{2,1,0:T(8,128)} %copy.48), calls=%async_computation.4 | async-start | bytes 1310720 | tf_op jit(solution)/shard_map/all_to_all | solution.py:363

commit v4 on v3

--- a/solution.py
+++ b/solution.py
@@ -264,7 +264,8 @@
 
     lat_held = jnp.pad(
         lat_of_slot.reshape(n_lev, slots_lev), ((0, 0), (0, spare)), constant_values=-1
-    ).reshape(1, -1)
+    )
+    lat_held = lat_held.reshape(n_lev, n_wave, some).transpose(1, 0, 2).reshape(1, -1)
     slots = lat_held.shape[1]
     lat_idx = jnp.arange(half, dtype=jnp.int32)[:, None]
     north = (lat_held == lat_idx).astype(jnp.float32)
@@ -284,9 +285,10 @@
         compiler_params=params,
         name="forward_rows",
     )(facts, rows_in, order)
-    fourier = fourier.reshape(some, fields, devices, 2 * span).transpose(2, 3, 1, 0)
-    arrived = exchange(fourier, BOTH).reshape(n_wave, n_lev, 2 * span * fields, some)
-    arrived = arrived.transpose(2, 1, 0, 3).reshape(2 * span * fields, slots)
+    fourier = lax.optimization_barrier(fourier.transpose(1, 0, 2).reshape(fields * some, columns))
+    fourier = lax.optimization_barrier(fourier.T).reshape(devices, 2 * span, fields, some)
+    arrived = exchange(fourier, BOTH).reshape(devices, 2 * span * fields, some)
+    arrived = arrived.transpose(1, 0, 2).reshape(2 * span * fields, slots)
     symmetric = jnp.einsum("cs,rs->cr", arrived, both, precision=HIGHEST) * lat_weight
     antisymmetric = jnp.einsum("cs,rs->cr", arrived, apart, precision=HIGHEST) * lat_weight
     symmetric = symmetric.reshape(span, 2 * fields, half)
@@ -333,10 +335,13 @@
         name="legendre_both",
     )(place, my_low, symmetric, antisymmetric, legendre, grow(vert_modes), grow(vert_back), rates)
 
-    by_slot = jnp.einsum("cfr,rs->cfs", even, both, precision=HIGHEST)
-    by_slot += jnp.einsum("cfr,rs->cfs", odd, apart, precision=HIGHEST)
-    by_slot = by_slot.reshape(2 * span * fields, n_lev, n_wave, some).transpose(2, 1, 0, 3)
-    returned = exchange(by_slot.reshape(devices, 2 * span, fields, some), BOTH)
+    turned = [
+        x.reshape(2 * span, fields, half).transpose(1, 0, 2).reshape(fields * 2 * span, half)
+        for x in (even, odd)
+    ]
+    by_slot = jnp.einsum("rs,cr->sc", both, turned[0], precision=HIGHEST)
+    by_slot += jnp.einsum("rs,cr->sc", apart, turned[1], precision=HIGHEST)
+    returned = exchange(by_slot.reshape(devices, some, fields, 2 * span), BOTH)
 
     pieces = lax.all_to_all(
         spec.reshape(n_lev, fields // n_lev, steps * WIDTH), "lev", split_axis=0, concat_axis=0, tiled=True
@@ -348,7 +353,7 @@
     )
     spectral = spectral[:, :modes_pad].reshape(ld, 2, modes_pad)
 
-    returned = returned.transpose(3, 2, 0, 1).reshape(some, fields, columns)
+    returned = returned.transpose(1, 2, 0, 3).reshape(some, fields, columns)
     values = pl.pallas_call(
         functools.partial(inverse_kernel, levels, outer, 1.0 / math.sqrt(waves)),
         out_shape=jax.ShapeDtypeStruct((some, levels * outer, INNER), jnp.float32),

time: 170 us -> 156 us (0.918)
  local copies, waits for them, and re-layouts: 44.4 us -> 30.4 us
    reshape x5 -> x8, local copies, waits for them, and re-layouts: 13.3 us -> 4.77 us  [the longest x1 3.27 us: body(): returned = returned.transpose(1, 2, 0, 3).reshape(some, fields, columns)]
    transpose x3 -> x4, local copies, waits for them, and re-layouts: 8.08 us -> 5.29 us  [the longest x1 3.02 us: body(): returned = returned.transpose(1, 2, 0, 3).reshape(some, fields, columns)]
    another operation x1 -> x2, local copies, waits for them, and re-layouts: 4.2 us -> 2.48 us  [exchange(): blocks.reshape(dense)]
  transfers between devices with their start and end apart: 5 -> 5, of which waited for: 4 -> 5; matrix products, arithmetic and copies ran while one was open for 9% -> 5% of each run, Pallas kernels for 0% -> 0%
where the time goes in v4:
time: 156 us; the launch traced here: 155 us
  waiting for transfers between devices  63.7 us (41%)
  Pallas kernels  31.3 us (20%)
  local copies, waits for them, and re-layouts  30.4 us (19%)
  starting transfers between devices  20.9 us (13%)
  matrix products  7.07 us (5%)
    all_to_all x2, waiting for transfers between devices, exchange(): lax.all_to_all(blocks.reshape(dense), axes, split_axis=0, concat_axis=0,...  29.9 us
    all_to_all x1, waiting for transfers between devices, body(): lax.all_to_all(values, 'wave', split_axis=0, concat_axis=0, tiled=True)  16.8 us
    all_to_all x1, waiting for transfers between devices, body(): lax.all_to_all(blocks, 'wave', split_axis=0, concat_axis=0, tiled=True)  15.5 us
    pallas_call x1, Pallas kernels, body(): pl.pallas_call(functools.partial(legendre_kernel, waves, used, span), out...  13.5 us
    pallas_call x1, Pallas kernels, body(): pl.pallas_call(functools.partial(inverse_kernel, levels, outer, 1.0 / mat...  9.49 us
    pallas_call x1, Pallas kernels, body(): pl.pallas_call(functools.partial(forward_kernel, levels, outer), out_shap...  8.36 us
    all_to_all x1, starting transfers between devices, body(): lax.all_to_all(blocks, 'wave', split_axis=0, concat_axis=0, tiled=True)  7.25 us
    all_to_all x2, starting transfers between devices, exchange(): lax.all_to_all(blocks.reshape(dense), axes, split_axis=0, concat_axis=0,...  6.69 us
  transfers between devices with their start and end apart: 5, of which 5 were waited for; matrix products, arithmetic and copies ran while one was open for 5% of the time, Pallas kernels for 0%

profile of v4, /device:TPU:0, one launch (start us, length us, event | category | flops | bytes accessed | tf_op | source)
XLA Modules:
  0.0 155.4 jit_solution(5162155915324108414)
XLA Ops:
  0.7 1.5 copy.43
  2.2 0.4 copy.44
  2.6 1.0 copy.45
  3.6 7.3 %all-to-all-start = ((f32[8,80,168]{2,1,0:T(8,128)}), f32[8,80,168]{2,1,0:T(8,128)S(1)}, u32[]{:S(2)}, u32[]{:S(2)}) async-start(f32[8,80,168]{2,1,0:T(8,128)} %copy.45), calls=%async_computation | async-start | bytes 1310720 | tf_op jit(solution)/shard_map/all_to_all | solution.py:259
  10.9 0.7 gather_fusion
  11.7 0.1 copy.48
  11.8 0.1 convert_element_type.54.wave_ref
  12.0 0.7 gather_fusion.1
  12.7 15.5 %all-to-all-done = f32[8,80,168]{2,1,0:T(8,128)S(1)} async-done(((f32[8,80,168]{2,1,0:T(8,128)}), f32[8,80,168]{2,1,0:T(8,128)S(1)}, u32[]{:S(2)}, u32[]{:S(2)}) %all-to-all-start) | async-done | bytes 430112 | tf_op jit(solution)/shard_map/all_to_all | solution.py:259
  28.2 0.4 copy.46
  28.6 0.3 reshape.222
  28.9 0.1 copy.63
  29.1 0.4 reshape.187.x_ref
  29.5 8.4 %forward_rows.1 = f32[20,8,640]{2,1,0:T(8,128)S(1)} custom-call(f32[3,20]{1,0:T(4,128)S(1)} %pad_maximum_fusion.facts, f32[20,96,64]{2,1,0:T(8,128)S(1)} %reshape.187.x_ref, f32[1,640]{1,0:T(1,128)S(1)} %convert_element_type.54.wave_ref), custom_call_target="tpu_custom_call" | custom-call | tf_op jit(solution)/shard_map/forward_rows/pallas_call | solution.py:280
  38.0 0.2 copy.50
  38.2 1.2 reshape_reshape.9
  39.5 3.9 %all-to-all-start.1 = ((f32[32,25,128]{2,1,0:T(8,128)}), f32[32,25,128]{2,1,0:T(8,128)S(1)}, u32[]{:S(2)}, u32[]{:S(2)}) async-start(f32[32,25,128]{2,1,0:T(8,128)} %reshape_reshape.9), calls=%async_computation.1 | async-start | bytes 1048576 | tf_op jit(solution)/shard_map/all_to_all | solution.py:226
  43.4 0.1 reshape.190
  43.7 0.1 eq.35
  44.2 14.6 %all-to-all-done.1 = f32[32,25,128]{2,1,0:T(8,128)S(1)} async-done(((f32[32,25,128]{2,1,0:T(8,128)}), f32[32,25,128]{2,1,0:T(8,128)S(1)}, u32[]{:S(2)}, u32[]{:S(2)}) %all-to-all-start.1) | async-done | bytes 409632 | tf_op jit(solution)/shard_map/all_to_all | solution.py:226
  58.7 3.2 %reshape_reshape.10 = f32[32,160,20]{2,1,0:T(8,128)S(1)} reshape(f32[32,25,128]{2,1,0:T(8,128)S(1)} %all-to-all-done.1) | data formatting | bytes 819200 | tf_op jit(solution)/shard_map/reshape;reshape | solution.py:290
  61.9 2.2 %copy.51 = f32[160,32,20]{0,2,1:T(8,128)} copy(f32[160,32,20]{2,0,1:T(8,128)S(1)} %bitcast.70) | data formatting | bytes 819200 | tf_op jit(solution)/shard_map/transpose | solution.py:291
  64.1 1.2 reshape.189
  65.3 2.4 %convolution_multiply_fusion = f32[160,320]{1,0:T(8,128)S(1)} fusion(f32[160,640]{0,1:T(8,128)S(1)} %reshape.189, s32[640]{0:T(1024)S(1)} %eq.35, s32[320]{0:T(512)S(1)} %iota_subtract_fusion, f32[320]{0:T(512)S(1)} %copy-done.2), kind=kOutput, calls=%fused_computation.3 | convolution fusion | flops 394291200 | bytes 619520 | tf_op jit(solution)/shard_map/cs,rs->cr/dot_general | solution.py:293
  67.7 2.4 %convolution_multiply_fusion.1 = f32[160,320]{1,0:T(8,128)S(1)} fusion(f32[160,640]{0,1:T(8,128)S(1)} %reshape.189, s32[640]{0:T(1024)S(1)} %eq.35, s32[320]{0:T(512)S(1)} %iota_subtract_fusion, f32[320]{0:T(512)S(1)} %copy-done.2), kind=kOutput, calls=%fused_computation.4 | convolution fusion | flops 394291200 | bytes 619520 | tf_op jit(solution)/shard_map/cs,rs->cr/dot_general | solution.py:292
  70.1 13.5 %legendre_both.1 = (f32[8,7040]{1,0:T(8,128)S(1)}, f32[10,16,320]{2,1,0:T(8,128)S(1)}, f32[10,16,320]{2,1,0:T(8,128)S(1)}) custom-call(s32[2]{0:T(128)S(1)} %pad_add_fusion.3.place, s32[40]{0:T(128)S(1)} %dynamic_slice.3.low, f32[10,16,320]{2,1,0:T(8,128)S(1)} %bitcast.67, f32[10,16,320]{2,1,0:T(8,128)S(1)} %bitcast.66, f32[320,25640]{1,0:T(8,128)} %leg_ref.1, ...), custom_call_target="tpu_custom_call" | custom-call | tf_op jit(solution)/shard_map/legendre_both/pallas_call | solution.py:308
  83.6 0.8 reshape.193
  84.4 3.4 %all-to-all-start.2 = ((f32[4,2,7040]{2,1,0:T(2,128)}), f32[4,2,7040]{2,1,0:T(2,128)S(1)}, u32[]{:S(2)}, u32[]{:S(2)}) async-start(f32[4,2,7040]{2,1,0:T(2,128)} %reshape.193), calls=%async_computation.2 | async-start | bytes 450560 | tf_op jit(solution)/shard_map/all_to_all | solution.py:346
  87.9 1.2 fusion
  89.1 1.2 convolution_add_fusion
  90.3 0.2 copy.56
  90.6 1.2 reshape_reshape.11
  91.8 1.6 %all-to-all-done.2 = f32[4,2,7040]{2,1,0:T(2,128)S(1)} async-done(((f32[4,2,7040]{2,1,0:T(2,128)}), f32[4,2,7040]{2,1,0:T(2,128)S(1)}, u32[]{:S(2)}, u32[]{:S(2)}) %all-to-all-start.2) | async-done | bytes 225312 | tf_op jit(solution)/shard_map/all_to_all | solution.py:346
  93.4 2.8 %all-to-all-start.3 = ((f32[32,25,128]{2,1,0:T(8,128)}), f32[32,25,128]{2,1,0:T(8,128)S(1)}, u32[]{:S(2)}, u32[]{:S(2)}) async-start(f32[32,25,128]{2,1,0:T(8,128)} %reshape_reshape.11), calls=%async_computation.3 | async-start | bytes 1048576 | tf_op jit(solution)/shard_map/all_to_all | solution.py:226
  96.2 15.3 %all-to-all-done.3 = f32[32,25,128]{2,1,0:T(8,128)S(1)} async-done(((f32[32,25,128]{2,1,0:T(8,128)}), f32[32,25,128]{2,1,0:T(8,128)S(1)}, u32[]{:S(2)}, u32[]{:S(2)}) %all-to-all-start.3) | async-done | bytes 409632 | tf_op jit(solution)/shard_map/all_to_all | solution.py:226
  111.5 3.2 %reshape.199 = f32[32,20,8,20]{3,2,1,0:T(8,128)S(1)} reshape(f32[32,25,128]{2,1,0:T(8,128)S(1)} %all-to-all-done.3) | data formatting | bytes 819200 | tf_op jit(solution)/shard_map/reshape | solution.py:227
  114.7 3.0 %copy.57 = f32[20,8,32,20]{3,2,1,0:T(8,128)} copy(f32[20,8,32,20]{3,1,0,2:T(8,128)S(1)} %bitcast.71) | data formatting | bytes 819200 | tf_op jit(solution)/shard_map/transpose | solution.py:356
  117.8 3.3 %reshape.200.f_ref = f32[20,8,640]{2,1,0:T(8,128)S(1)} reshape(f32[20,8,32,20]{3,2,1,0:T(8,128)} %copy.57) | data formatting | bytes 819200 | tf_op jit(solution)/shard_map/reshape | solution.py:356
  121.0 9.5 %inverse_rows.1 = f32[20,96,64]{2,1,0:T(8,128)S(1)} custom-call(f32[3,20]{1,0:T(4,128)S(1)} %pad_maximum_fusion.facts, f32[20,8,640]{2,1,0:T(8,128)S(1)} %reshape.200.f_ref, f32[1,640]{1,0:T(1,128)S(1)} %convert_element_type.54.wave_ref), custom_call_target="tpu_custom_call" | custom-call | tf_op jit(solution)/shard_map/inverse_rows/pallas_call | solution.py:357
  130.5 0.3 reshape.201
  130.9 0.5 reshape.202
  131.5 1.0 copy.59
  132.5 3.5 %all-to-all-start.4 = ((f32[8,80,168]{2,1,0:T(8,128)}), f32[8,80,168]{2,1,0:T(8,128)S(1)}, u32[]{:S(2)}, u32[]{:S(2)}) async-start(f32[8,80,168]{2,1,0:T(8,128)} %copy.59), calls=%async_computation.4 | async-start | bytes 1310720 | tf_op jit(solution)/shard_map/all_to_all | solution.py:368
  136.1 0.7 fusion.9
  136.8 16.8 %all-to-all-done.4 = f32[8,80,168]{2,1,0:T(8,128)S(1)} async-done(((f32[8,80,168]{2,1,0:T(8,128)}), f32[8,80,168]{2,1,0:T(8,128)S(1)}, u32[]{:S(2)}, u32[]{:S(2)}) %all-to-all-start.4) | async-done | bytes 430112 | tf_op jit(solution)/shard_map/all_to_all | solution.py:368
  153.6 0.4 copy.60
  154.0 0.4 copy.61
  154.4 1.0 copy.62
  (44 shorter events, 1.2 us)
Async XLA Ops:
  0.6 11.4 %copy-start = (s32[640]{0:T(1024)S(1)}, s32[640]{0:T(1024)}, u32[]{:S(2)}) copy-start(s32[640]{0:T(1024)} %param.10) | copy-start | bytes 7684
  0.6 10.3 %copy-start.1 = (s32[640]{0:T(1024)S(1)}, s32[640]{0:T(1024)}, u32[]{:S(2)}) copy-start(s32[640]{0:T(1024)} %param.11) | copy-start | bytes 7684
  0.7 10.9 %copy-start.3 = (s32[320]{0:T(512)S(1)}, s32[320]{0:T(512)}, u32[]{:S(2)}) copy-start(s32[320]{0:T(512)} %param.12) | copy-start | bytes 3844
  3.6 24.5 %all-to-all-start = ((f32[8,80,168]{2,1,0:T(8,128)}), f32[8,80,168]{2,1,0:T(8,128)S(1)}, u32[]{:S(2)}, u32[]{:S(2)}) async-start(f32[8,80,168]{2,1,0:T(8,128)} %copy.45), calls=%async_computation | async-start | bytes 1310720 | tf_op jit(solution)/shard_map/all_to_all | solution.py:259
  37.8 5.7 %copy-start.6 = (f32[4]{0:T(128)S(1)}, f32[4]{0:T(128)}, u32[]{:S(2)}) copy-start(f32[4]{0:T(128)} %param.17) | copy-start | bytes 52
  37.8 6.0 %copy-start.4 = (f32[4,4]{1,0:T(4,128)S(1)}, f32[4,4]{1,0:T(4,128)}, u32[]{:S(2)}) copy-start(f32[4,4]{1,0:T(4,128)} %param.16) | copy-start | bytes 196
  37.8 6.0 %copy-start.5 = (f32[4,4]{1,0:T(4,128)S(1)}, f32[4,4]{1,0:T(4,128)}, u32[]{:S(2)}) copy-start(f32[4,4]{1,0:T(4,128)} %param.15) | copy-start | bytes 196
  39.5 19.2 %all-to-all-start.1 = ((f32[32,25,128]{2,1,0:T(8,128)}), f32[32,25,128]{2,1,0:T(8,128)S(1)}, u32[]{:S(2)}, u32[]{:S(2)}) async-start(f32[32,25,128]{2,1,0:T(8,128)} %reshape_reshape.9), calls=%async_computation.1 | async-start | bytes 1048576 | tf_op jit(solution)/shard_map/all_to_all | solution.py:226
  61.9 3.4 %copy-start.2 = (f32[320]{0:T(512)S(1)}, f32[320]{0:T(512)}, u32[]{:S(2)}) copy-start(f32[320]{0:T(512)} %param.14) | copy-start | bytes 3844
  84.4 9.0 %all-to-all-start.2 = ((f32[4,2,7040]{2,1,0:T(2,128)}), f32[4,2,7040]{2,1,0:T(2,128)S(1)}, u32[]{:S(2)}, u32[]{:S(2)}) async-start(f32[4,2,7040]{2,1,0:T(2,128)} %reshape.193), calls=%async_computation.2 | async-start | bytes 450560 | tf_op jit(solution)/shard_map/all_to_all | solution.py:346
  93.4 18.2 %all-to-all-start.3 = ((f32[32,25,128]{2,1,0:T(8,128)}), f32[32,25,128]{2,1,0:T(8,128)S(1)}, u32[]{:S(2)}, u32[]{:S(2)}) async-start(f32[32,25,128]{2,1,0:T(8,128)} %reshape_reshape.11), calls=%async_computation.3 | async-start | bytes 1048576 | tf_op jit(solution)/shard_map/all_to_all | solution.py:226
  132.5 21.1 %all-to-all-start.4 = ((f32[8,80,168]{2,1,0:T(8,128)}), f32[8,80,168]{2,1,0:T(8,128)S(1)}, u32[]{:S(2)}, u32[]{:S(2)}) async-start(f32[8,80,168]{2,1,0:T(8,128)} %copy.59), calls=%async_computation.4 | async-start | bytes 1310720 | tf_op jit(solution)/shard_map/all_to_all | solution.py:368
